TPU v7x, 256 devices: a whole 4x4x8 slice. The times are simulated.
256 devices in a mesh: branch: 16 (over z, core), grid: 16 (over y, x).
Axes of the slice: x: 4, y: 4, z: 8, core: 2. Of those that a mesh axis runs over, the one named last changes fastest.
Arguments:
- sigma_top: float32 [8192, 8192], P('grid', 'branch'), as said below
- mid_struct: int32 [16, 12], P('branch'), may hold values from 0 to 31, as said below
- leaf_struct: int32 [16, 6], P('branch'), may hold values from 0 to 11, as said below
- mid_inv: float32 [16, 256, 256], P('branch'), as said below
- mid_off: float32 [16, 12, 256, 256], P('branch'), may hold values from -0.375 to 0.375
- leaf_inv: float32 [16, 256, 256], P('branch'), as said below
- leaf_off: float32 [16, 7, 256, 256], P('branch'), may hold values from -0.375 to 0.375
Outputs:
- sigma_mid_off: float32 [16, 12, 256, 256], P('branch', None, 'grid')
- sigma_mid_diag: float32 [16, 256, 256], P('branch')
- sigma_leaf_off: float32 [16, 12, 256, 256], P('branch', None, 'grid')
- sigma_leaf_parent: float32 [16, 256, 256], P('branch')
- sigma_leaf_diag: float32 [16, 256, 256], P('branch')
Inputs may be any that keep to these rules, and one draw needn't show every extreme that they name: sigma_top is exactly symmetric. `mid_struct`: each row holds 12 different top row blocks in increasing order; the last is always 32 - 1. `leaf_struct`: each row holds 6 different positions in increasing order; the last is always 12 - 1. `mid_inv`: lower triangular with a positive diagonal. `leaf_inv`: lower triangular with a positive diagonal.
All inputs are finite; a program needn't handle non-finite values.
Results may differ from a plain program's by a relative error of at most 0.0003.
Values sent between devices are 32-bit elements; how exact they have to be, the bound alone decides.
A program may use at most 128 MiB of HBM per device.

v0:
```python
import jax
import jax.numpy as jnp
from jax import lax
from jax.sharding import PartitionSpec as P


def contract_rows(left, right):
    return jnp.einsum("kab,kac->bc", left, right, precision=lax.Precision.HIGHEST)


def fold_blocks(carry, piece, struct, block, add_block):
    count = piece.shape[1] // block

    def step(index, acc):
        match = struct == index
        found = jnp.any(match)
        where = jnp.argmax(match.astype(jnp.int32))
        column = lax.dynamic_slice_in_dim(piece, index * block, block, 1)
        return lax.cond(
            found, lambda inner: add_block(inner, column, where), lambda inner: inner, acc
        )

    return lax.fori_loop(0, count, step, carry)


def on_device(sigma_top, mid_struct, leaf_struct, mid_inv, mid_off, leaf_inv, leaf_off):
    highest = lax.Precision.HIGHEST
    grid_count = lax.axis_size("grid")
    grid_pos = lax.axis_index("grid")
    block = mid_inv.shape[-1]
    s_count = mid_struct.shape[-1]
    slab_rows = sigma_top.shape[0]
    owned = slab_rows // block
    struct = mid_struct[0]
    leaf_pos = leaf_struct[0]
    minv = mid_inv[0]
    linv = leaf_inv[0]
    upper = jnp.einsum("kab,bc->kac", mid_off[0], minv, precision=highest)
    leaf_v = jnp.einsum("kab,bc->kac", leaf_off[0], linv, precision=highest)
    first = leaf_v[0]
    place = (leaf_pos[:, None] == jnp.arange(s_count, dtype=jnp.int32)[None, :]).astype(jnp.float32)
    spread = jnp.einsum("ti,tab->iab", place, leaf_v[1:], precision=highest)
    both = jnp.concatenate([upper, spread], axis=2)
    share_rows = block // grid_count
    own_ids = grid_pos * owned + jnp.arange(owned, dtype=jnp.int32)
    pick = (own_ids[:, None] == struct[None, :]).astype(jnp.float32)
    weights = jnp.einsum("ai,ibc->abc", pick, both, precision=highest).reshape(slab_rows, 2 * block)

    def add_left(acc, column, where):
        term = lax.dot_general(column, weights, (((0,), (0,)), ((), ())), precision=highest)
        current = lax.dynamic_index_in_dim(acc, where, 0, keepdims=False)
        return lax.dynamic_update_index_in_dim(acc, current + term, where, 0)

    empty_cols = jnp.zeros((s_count, block, 2 * block), jnp.float32)
    chosen = fold_blocks(
        empty_cols, lax.all_gather(sigma_top, "branch", axis=1, tiled=True), struct, block, add_left
    )
    summed = lax.psum(chosen, "grid")
    mid_all = -summed[:, :, :block]
    far_all = summed[:, :, block:]
    mid_diag = jnp.dot(minv.T, minv, precision=highest) - contract_rows(upper, mid_all)
    zpar = jnp.dot(mid_diag, first, precision=highest) + contract_rows(mid_all, spread)
    zall = jnp.einsum("kab,bc->kac", mid_all, first, precision=highest) + far_all
    leaf_diag = (
        jnp.dot(linv.T, linv, precision=highest)
        + jnp.dot(first.T, zpar, precision=highest)
        + contract_rows(spread, zall)
    )
    mid_col = lax.dynamic_slice_in_dim(mid_all, grid_pos * share_rows, share_rows, 1)
    zstr = lax.dynamic_slice_in_dim(zall, grid_pos * share_rows, share_rows, 1)
    marks = jnp.sum(place, axis=0)
    leaf_col = -zstr * marks[:, None, None]
    return (mid_col[None], mid_diag[None], leaf_col[None], (-zpar)[None], leaf_diag[None])


def solution(mesh):
    in_specs = (
        P("grid", "branch"),
        P("branch", None),
        P("branch", None),
        P("branch", None, None),
        P("branch", None, None, None),
        P("branch", None, None),
        P("branch", None, None, None),
    )
    out_specs = (
        P("branch", None, "grid", None),
        P("branch", None, None),
        P("branch", None, "grid", None),
        P("branch", None, None),
        P("branch", None, None),
    )
    return jax.shard_map(
        on_device, mesh=mesh, in_specs=in_specs, out_specs=out_specs, check_vma=False
    )
```

profile of v0, /device:TPU:1, one launch (start us, length us, event | category | flops | bytes accessed | tf_op | source)
XLA Modules:
  0.0 408.0 jit_solution(12338652225582067221)
XLA Ops:
  12.6 4.2 %fusion.7 = f32[12,256,256]{2,0,1:T(8,128)} fusion(f32[6,256,256]{2,1,0:T(8,128)S(1)} %slice.16, s32[6]{0:T(128)S(1)} %bitcast.69), kind=kOutput, calls=%fused_computation.14 | convolution fusion | flops 56623176 | bytes 4718616 | tf_op jit(solution)/shard_map/ti,tab->iab/dot_general | solution.py:42
  16.9 5.0 %copy.21 = f32[12,256,256]{1,2,0:T(8,128)} copy(f32[12,256,256]{2,0,1:T(8,128)} %fusion.7) | data formatting | bytes 6291456 | tf_op jit(solution)/shard_map/ti,tab->iab/dot_general | solution.py:42
  26.6 3.5 pad_maximum_fusion
  30.1 9.7 %copy.22 = f32[12,256,512]{2,0,1:T(8,128)} copy(f32[12,256,512]{1,2,0:T(8,128)} %pad_maximum_fusion) | data formatting | bytes 12582912 | tf_op jit(solution)/shard_map/concatenate | solution.py:43
  39.8 6.6 %fusion.27 = f32[2,256,512]{2,0,1:T(2,128)S(1)} fusion(f32[12,256,512]{2,0,1:T(8,128)} %copy.22, s32[12]{0:T(128)S(1)} %bitcast.67, s32[2]{0:T(128)S(1)} %iota_add_fusion), kind=kOutput, calls=%fused_computation.44 | convolution fusion | flops 37748760 | bytes 7340088 | tf_op jit(solution)/shard_map/ai,ibc->abc/dot_general | solution.py:47
  46.7 62.8 %all-gather.2.cloned.1.call-done = f32[512,8192]{1,0:T(8,128)} async-done(((f32[512,512]{1,0:T(8,128)}), f32[512,8192]{1,0:T(8,128)}) %all-gather.2.cloned.1.call-update) | async-done | bytes 16777232 | tf_op jit(solution)/shard_map/all_gather | solution.py:56
  109.5 3.4 broadcast_in_dim.27
  112.9 134.2 %while.16 = (s32[]{:T(128)}, f32[12,256,512]{2,1,0:T(8,128)}, s32[12]{0:T(128)S(1)}, f32[512,8192]{1,0:T(8,128)}, f32[512,512]{1,0:T(8,128)S(1)}, /*index=5*/s32[]{:T(128)}) while((s32[]{:T(128)}, f32[12,256,512]{2,1,0:T(8,128)}, s32[12]{0:T(128)S(1)}, f32[512,8192]{1,0:T(8,128)}, f32[512,512]{1,0:T(8,128)S(1)}, /*index=5*/s32[]{:T(128)}) %tuple.64), condition=%wide.region_5.6_spmd, body=%wide.region_0.5_spmd.sunk | while | flops 805437568 | bytes 3670343 | solution.py:23
  114.9 6.0 %conditional.2 = (f32[12,256,512]{2,1,0:T(8,128)}) conditional(s32[]{:T(128)} %convert_element_type.26, f32[12,256,512]{2,1,0:T(8,128)} %get-tuple-element.216, (s32[]{:T(128)}, f32[12,256,512]{2,1,0:T(8,128)}, s32[]{:T(128)}, f32[512,8192]{1,0:T(8,128)}, f32[512,512]{1,0:T(8,128)S(1)}) %tuple.53), branch_computations={%region_3.3_spmd, %region_4.4_spmd} | conditional | flops 805437440 | bytes 3670116 | solution.py:19
  124.7 5.9 %conditional.2 = (f32[12,256,512]{2,1,0:T(8,128)}) conditional(s32[]{:T(128)} %convert_element_type.26, f32[12,256,512]{2,1,0:T(8,128)} %get-tuple-element.216, (s32[]{:T(128)}, f32[12,256,512]{2,1,0:T(8,128)}, s32[]{:T(128)}, f32[512,8192]{1,0:T(8,128)}, f32[512,512]{1,0:T(8,128)S(1)}) %tuple.53), branch_computations={%region_3.3_spmd, %region_4.4_spmd} | conditional | flops 805437440 | bytes 3670116 | solution.py:19
  136.6 6.0 %conditional.2 = (f32[12,256,512]{2,1,0:T(8,128)}) conditional(s32[]{:T(128)} %convert_element_type.26, f32[12,256,512]{2,1,0:T(8,128)} %get-tuple-element.216, (s32[]{:T(128)}, f32[12,256,512]{2,1,0:T(8,128)}, s32[]{:T(128)}, f32[512,8192]{1,0:T(8,128)}, f32[512,512]{1,0:T(8,128)S(1)}) %tuple.53), branch_computations={%region_3.3_spmd, %region_4.4_spmd} | conditional | flops 805437440 | bytes 3670116 | solution.py:19
  156.3 5.9 %conditional.2 = (f32[12,256,512]{2,1,0:T(8,128)}) conditional(s32[]{:T(128)} %convert_element_type.26, f32[12,256,512]{2,1,0:T(8,128)} %get-tuple-element.216, (s32[]{:T(128)}, f32[12,256,512]{2,1,0:T(8,128)}, s32[]{:T(128)}, f32[512,8192]{1,0:T(8,128)}, f32[512,512]{1,0:T(8,128)S(1)}) %tuple.53), branch_computations={%region_3.3_spmd, %region_4.4_spmd} | conditional | flops 805437440 | bytes 3670116 | solution.py:19
  164.2 6.0 %conditional.2 = (f32[12,256,512]{2,1,0:T(8,128)}) conditional(s32[]{:T(128)} %convert_element_type.26, f32[12,256,512]{2,1,0:T(8,128)} %get-tuple-element.216, (s32[]{:T(128)}, f32[12,256,512]{2,1,0:T(8,128)}, s32[]{:T(128)}, f32[512,8192]{1,0:T(8,128)}, f32[512,512]{1,0:T(8,128)S(1)}) %tuple.53), branch_computations={%region_3.3_spmd, %region_4.4_spmd} | conditional | flops 805437440 | bytes 3670116 | solution.py:19
  183.9 6.0 %conditional.2 = (f32[12,256,512]{2,1,0:T(8,128)}) conditional(s32[]{:T(128)} %convert_element_type.26, f32[12,256,512]{2,1,0:T(8,128)} %get-tuple-element.216, (s32[]{:T(128)}, f32[12,256,512]{2,1,0:T(8,128)}, s32[]{:T(128)}, f32[512,8192]{1,0:T(8,128)}, f32[512,512]{1,0:T(8,128)S(1)}) %tuple.53), branch_computations={%region_3.3_spmd, %region_4.4_spmd} | conditional | flops 805437440 | bytes 3670116 | solution.py:19
  195.8 6.0 %conditional.2 = (f32[12,256,512]{2,1,0:T(8,128)}) conditional(s32[]{:T(128)} %convert_element_type.26, f32[12,256,512]{2,1,0:T(8,128)} %get-tuple-element.216, (s32[]{:T(128)}, f32[12,256,512]{2,1,0:T(8,128)}, s32[]{:T(128)}, f32[512,8192]{1,0:T(8,128)}, f32[512,512]{1,0:T(8,128)S(1)}) %tuple.53), branch_computations={%region_3.3_spmd, %region_4.4_spmd} | conditional | flops 805437440 | bytes 3670116 | solution.py:19
  203.7 6.0 %conditional.2 = (f32[12,256,512]{2,1,0:T(8,128)}) conditional(s32[]{:T(128)} %convert_element_type.26, f32[12,256,512]{2,1,0:T(8,128)} %get-tuple-element.216, (s32[]{:T(128)}, f32[12,256,512]{2,1,0:T(8,128)}, s32[]{:T(128)}, f32[512,8192]{1,0:T(8,128)}, f32[512,512]{1,0:T(8,128)S(1)}) %tuple.53), branch_computations={%region_3.3_spmd, %region_4.4_spmd} | conditional | flops 805437440 | bytes 3670116 | solution.py:19
  211.6 6.0 %conditional.2 = (f32[12,256,512]{2,1,0:T(8,128)}) conditional(s32[]{:T(128)} %convert_element_type.26, f32[12,256,512]{2,1,0:T(8,128)} %get-tuple-element.216, (s32[]{:T(128)}, f32[12,256,512]{2,1,0:T(8,128)}, s32[]{:T(128)}, f32[512,8192]{1,0:T(8,128)}, f32[512,512]{1,0:T(8,128)S(1)}) %tuple.53), branch_computations={%region_3.3_spmd, %region_4.4_spmd} | conditional | flops 805437440 | bytes 3670116 | solution.py:19
  221.4 6.0 %conditional.2 = (f32[12,256,512]{2,1,0:T(8,128)}) conditional(s32[]{:T(128)} %convert_element_type.26, f32[12,256,512]{2,1,0:T(8,128)} %get-tuple-element.216, (s32[]{:T(128)}, f32[12,256,512]{2,1,0:T(8,128)}, s32[]{:T(128)}, f32[512,8192]{1,0:T(8,128)}, f32[512,512]{1,0:T(8,128)S(1)}) %tuple.53), branch_computations={%region_3.3_spmd, %region_4.4_spmd} | conditional | flops 805437440 | bytes 3670116 | solution.py:19
  231.3 6.0 %conditional.2 = (f32[12,256,512]{2,1,0:T(8,128)}) conditional(s32[]{:T(128)} %convert_element_type.26, f32[12,256,512]{2,1,0:T(8,128)} %get-tuple-element.216, (s32[]{:T(128)}, f32[12,256,512]{2,1,0:T(8,128)}, s32[]{:T(128)}, f32[512,8192]{1,0:T(8,128)}, f32[512,512]{1,0:T(8,128)S(1)}) %tuple.53), branch_computations={%region_3.3_spmd, %region_4.4_spmd} | conditional | flops 805437440 | bytes 3670116 | solution.py:19
  241.2 5.9 %conditional.2 = (f32[12,256,512]{2,1,0:T(8,128)}) conditional(s32[]{:T(128)} %convert_element_type.26, f32[12,256,512]{2,1,0:T(8,128)} %get-tuple-element.216, (s32[]{:T(128)}, f32[12,256,512]{2,1,0:T(8,128)}, s32[]{:T(128)}, f32[512,8192]{1,0:T(8,128)}, f32[512,512]{1,0:T(8,128)S(1)}) %tuple.53), branch_computations={%region_3.3_spmd, %region_4.4_spmd} | conditional | flops 805437440 | bytes 3670116 | solution.py:19
  249.8 128.2 %all-reduce.2.cloned.1.call-done = f32[12,256,512]{2,1,0:T(8,128)} async-done(((f32[12,256,512]{2,1,0:T(8,128)}), f32[12,256,512]{2,1,0:T(8,128)}) %all-reduce.2.cloned.1.call-update) | async-done | bytes 6291472 | tf_op jit(solution)/shard_map/psum | solution.py:58
  377.9 4.8 %convolution_bitcast_fusion.2 = f32[256,256]{1,0:T(8,128)S(1)} fusion(f32[12,256,256]{1,2,0:T(8,128)S(1)} %copy-done.5, f32[12,256,512]{2,1,0:T(8,128)} %all-reduce.2.cloned.1.call-done), kind=kOutput, calls=%fused_computation.25 | convolution fusion | flops 2416705536 | bytes 6553600 | tf_op jit(solution)/shard_map/kab,kac->bc/dot_general | solution.py:8
  383.4 3.9 slice_add_fusion
  390.1 5.4 %convolution_bitcast_fusion.1 = f32[256,256]{1,0:T(8,128)S(1)} fusion(f32[12,256,256]{1,2,0:T(8,128)S(1)} %copy-done.3, f32[12,256,512]{2,1,0:T(8,128)S(1)} %copy-done.6), kind=kOutput, calls=%fused_computation.24 | convolution fusion | flops 2416705536 | bytes 6553600 | tf_op jit(solution)/shard_map/kab,kac->bc/dot_general | solution.py:8
  (152 shorter events, 111.2 us)
Async XLA Ops:
  7.2 14.7 %copy-start = (f32[1,12,256,256]{3,2,1,0:T(8,128)S(1)}, f32[1,12,256,256]{3,2,1,0:T(8,128)}, u32[]{:S(2)}) copy-start(f32[1,12,256,256]{3,2,1,0:T(8,128)} %param.15) | copy-start | bytes 9437188
  7.2 102.3 %all-gather.2.cloned.1.call-start = ((), (), s32[]{:S(2)}) async-start(), calls=%async_computation | async-start | bytes 17825792 | tf_op jit(solution)/shard_map/all_gather | solution.py:56
  7.9 370.0 %all-reduce.2.cloned.1.call-start = ((), (), s32[]{:S(2)}) async-start(), calls=%async_computation.1 | async-start | bytes 12582912 | tf_op jit(solution)/shard_map/psum | solution.py:58
  8.0 4.7 %copy-start.12 = (s32[1,6]{1,0:T(1,128)S(1)}, s32[1,6]{1,0:T(1,128)}, u32[]{:S(2)}) copy-start(s32[1,6]{1,0:T(1,128)} %param.13) | copy-start | bytes 76
  11.2 1.2 copy-start.7
  16.9 5.0 %copy-start.8 = (f32[1,256,256]{2,1,0:T(8,128)S(1)}, f32[1,256,256]{2,1,0:T(8,128)}, u32[]{:S(2)}) copy-start(f32[1,256,256]{2,1,0:T(8,128)} %param.14) | copy-start | bytes 786436
  21.9 4.7 %copy-start.2 = (f32[12,256,256]{1,2,0:T(8,128)S(1)}, f32[12,256,256]{1,2,0:T(8,128)}, u32[]{:S(2)}) copy-start(f32[12,256,256]{1,2,0:T(8,128)} %copy.21) | copy-start | bytes 9437188
  24.9 1.7 copy-start.4
  30.1 9.7 %copy-start.11 = (s32[1,12]{1,0:T(1,128)S(1)}, s32[1,12]{1,0:T(1,128)}, u32[]{:S(2)}) copy-start(s32[1,12]{1,0:T(1,128)} %param.12) | copy-start | bytes 148
  247.2 130.8 %copy-start.5 = (f32[12,256,256]{1,2,0:T(8,128)S(1)}, f32[12,256,256]{1,2,0:T(8,128)}, u32[]{:S(2)}) copy-start(f32[12,256,256]{1,2,0:T(8,128)} %copy-done.4) | copy-start | bytes 9437188
  377.9 5.4 %copy-start.6 = (f32[12,256,512]{2,1,0:T(8,128)S(1)}, f32[12,256,512]{2,1,0:T(8,128)}, u32[]{:S(2)}) copy-start(f32[12,256,512]{2,1,0:T(8,128)} %all-reduce.2.cloned.1.call-done) | copy-start | bytes 18874372
  383.3 12.2 %copy-start.10 = (f32[256,256]{1,0:T(8,128)}, f32[256,256]{1,0:T(8,128)S(1)}, u32[]{:S(2)}) copy-start(f32[256,256]{1,0:T(8,128)S(1)} %convolution_subtract_fusion) | copy-start | bytes 786436
  383.4 3.9 copy-start.3
  390.1 7.5 %copy-start.9 = (f32[256,256]{1,0:T(8,128)S(1)}, f32[256,256]{1,0:T(8,128)}, u32[]{:S(2)}) copy-start(f32[256,256]{1,0:T(8,128)} %fusion.18) | copy-start | bytes 786436
  397.6 3.6 copy-start.1
Sparse Core Ops, SparseCore 0:
  9.9 99.5 all-gather.1
  247.3 130.5 all-reduce.1
where the time goes:
time: 410 us; the launch traced here: 408 us
  waiting for transfers between devices  192 us (47%)
  matrix products  75.8 us (18%)
  other arithmetic  46.6 us (11%)
  loops' own time  45.2 us (11%)
  local copies, waits for them, and re-layouts  34.5 us (8%)
  between operations  14.2 us (3%)
    psum x1, waiting for transfers between devices, on_device(): summed = lax.psum(chosen, 'grid')  128 us
    all_gather x1, waiting for transfers between devices, on_device(): lax.all_gather(sigma_top, 'branch', axis=1, tiled=True)  62.8 us
    dot_general x12, matrix products, add_left(): lax.dot_general(column, weights, (((0,), (0,)), ((), ())), precision=high...  35 us
    another operation x32, loops' own time, step(): lax.cond(found, lambda inner: add_block(inner, column, where), lambda inn...  23.8 us
    another operation x1, loops' own time, fold_blocks(): return lax.fori_loop(0, count, step, carry)  21.4 us
    another operation x32, other arithmetic, step(): where = jnp.argmax(match.astype(jnp.int32))  20.9 us
    reduce_or x32, other arithmetic, step(): found = jnp.any(match)  20.2 us
    dot_general x3, matrix products, contract_rows(): jnp.einsum('kab,kac->bc', left, right, precision=lax.Precision.HIGHEST)  13 us
  transfers between devices with their start and end apart: 2, of which 2 were waited for; matrix products, arithmetic and copies ran while one was open for 9% of the time, Pallas kernels for 0%

commit v1 on v0

v1 whole, which is shorter than its diff:
```python
import functools

import jax
import jax.numpy as jnp
from jax import lax
from jax.experimental import pallas as pl
from jax.experimental.pallas import tpu as pltpu
from jax.sharding import PartitionSpec as P

MESH = pl.DeviceIdType.MESH
F32 = jnp.float32
BF16 = jnp.bfloat16
BS = 256
NS1 = 12
NS2 = 6
SIDE = 4
RING = 8
SUB = BS // SIDE
SLICE = 16
SLOTS = 17
PIECES = ((0, 4), (4, 4), (8, 4), (12, 5))
ROWS = NS1 * SUB
OUTS = NS1 + NS2


def split(value):
    high = value.astype(BF16)
    return high, (value - high.astype(F32)).astype(BF16)


def product(left, right, dims=(((1,), (0,)), ((), ()))):
    def one(a, b):
        return lax.dot_general(a, b, dims, preferred_element_type=F32)
    return one(left[0], right[0]) + (one(left[0], right[1]) + one(left[1], right[0]))


def product_t(left, right):
    return product(left, right, (((0,), (0,)), ((), ())))


def kernel(
    struct, leaf, sigma, minv_hbm, moff_hbm, linv_hbm, loff_hbm,
    mid_out, diag_out, leaf_out, parent_out, leaf_diag_out,
    packed, extra, gathered, moff, loff, first_raw, minv, linv, vblocks, v0_hi, v0_lo, base,
    w_hi, w_lo, wt_hi, wt_lo, a_hi, a_lo, ysum, ysend, yrecv, ycomb, gsend, grecv, gcomb, gred, gexch, gall,
    load_sem, pack_send, pack_recv, extra_send, extra_recv, z_send, right_recv, left_recv,
    pair_send, pair_recv, y_send_sem, y_recv_sem, g_send_sem, g_recv_sem,
):
    branch = lax.axis_index("branch")
    grid = lax.axis_index("grid")
    z, core = branch // 2, branch % 2
    y, x = grid // SIDE, grid % SIDE

    def slots(which_core, source, slot, size=None):
        start = (which_core * RING + source) * SLOTS + slot
        return gathered.at[start] if size is None else gathered.at[pl.ds(start, size)]

    def at_grid(index):
        return {"branch": branch, "grid": index}

    def at_branch(index):
        return {"branch": index, "grid": grid}

    up = at_branch(lax.rem(z + 1, RING) * 2 + core)
    down = at_branch(lax.rem(z + RING - 1, RING) * 2 + core)
    pair = at_branch(z * 2 + (1 - core))
    around = (
        (at_grid(y * SIDE + lax.rem(x + 1, SIDE)), at_grid(y * SIDE + lax.rem(x + SIDE - 1, SIDE))),
        (at_grid(lax.rem(y + 1, SIDE) * SIDE + x), at_grid(lax.rem(y + SIDE - 1, SIDE) * SIDE + x)),
    )
    place = (x, y)

    row_c = pl.multiple_of(y * SUB, SUB)
    loads = [
        pltpu.make_async_copy(minv_hbm.at[0], minv, load_sem.at[0]),
        pltpu.make_async_copy(linv_hbm.at[0], linv, load_sem.at[1]),
        pltpu.make_async_copy(loff_hbm.at[0, 0], first_raw, load_sem.at[2]),
        pltpu.make_async_copy(moff_hbm.at[0, :, pl.ds(row_c, SUB), :], moff.at[0], load_sem.at[3]),
        pltpu.make_async_copy(loff_hbm.at[0, pl.ds(1, NS2), pl.ds(row_c, SUB), :], loff.at[0], load_sem.at[4]),
    ]
    for m in range(SIDE):
        row_r = pl.multiple_of(m * SUB + x * SLICE, SLICE)
        into = pl.ds(m * SLICE, SLICE)
        loads.append(pltpu.make_async_copy(
            moff_hbm.at[0, :, pl.ds(row_r, SLICE), :], moff.at[1, :, into, :], load_sem.at[5 + m]))
        loads.append(pltpu.make_async_copy(
            loff_hbm.at[0, pl.ds(1, NS2), pl.ds(row_r, SLICE), :], loff.at[1, :, into, :], load_sem.at[9 + m]))
    for load in loads:
        load.start()

    barrier = pltpu.get_barrier_semaphore()

    def greet(step, carry):
        pl.semaphore_signal(
            barrier, inc=1, device_id=at_grid(lax.rem(grid + step, SIDE * SIDE)), device_id_type=MESH)
        return carry

    lax.fori_loop(1, SIDE * SIDE, greet, 0)
    for other in (up, down, pair):
        pl.semaphore_signal(barrier, inc=1, device_id=other, device_id_type=MESH)

    flip = (grid > branch).astype(jnp.int32)
    lane = lax.broadcasted_iota(jnp.int32, (BS, 128), 1)
    for half in range(2):
        one = sigma[0:BS, pl.ds(pl.multiple_of(flip * BS + half * 128, 128), 128)]
        two = sigma[BS:2 * BS, pl.ds(pl.multiple_of((1 - flip) * BS + half * 128, 128), 128)]
        even = jnp.where(lane < SUB, one, pltpu.roll(two, SUB, 1))
        odd = jnp.where(lane < SUB, pltpu.roll(one, SUB, 1), two)
        for side, value in ((2 * half, even), (2 * half + 1, odd)):
            for m in range(SIDE):
                for xx in range(SIDE):
                    start = m * SUB + xx * SLICE
                    packed[side * SIDE + xx, m * SLICE:(m + 1) * SLICE, :] = value[start:start + SLICE, :]

    @pl.when(grid == branch)
    def _():
        for half in range(2):
            value = sigma[0:BS, BS + half * 128:BS + (half + 1) * 128]
            for side, turned in ((2 * half, value), (2 * half + 1, pltpu.roll(value, SUB, 1))):
                for m in range(SIDE):
                    for xx in range(SIDE):
                        start = m * SUB + xx * SLICE
                        extra[side * SIDE + xx, m * SLICE:(m + 1) * SLICE, :] = turned[start:start + SLICE, :]

    pl.semaphore_wait(barrier, SIDE * SIDE + 2)

    pltpu.make_async_copy(packed.at[grid], slots(core, z, grid), pack_recv.at[grid // SIDE]).start()

    def hand_out(step, carry):
        to = lax.rem(grid + step, SIDE * SIDE)
        pltpu.make_async_remote_copy(
            src_ref=packed.at[to], dst_ref=slots(core, z, grid), send_sem=pack_send,
            recv_sem=pack_recv.at[grid // SIDE], device_id=at_grid(to), device_id_type=MESH).start()
        return carry

    lax.fori_loop(1, SIDE * SIDE, hand_out, 0)

    @pl.when(grid == branch)
    def _():
        pltpu.make_async_copy(extra.at[grid], slots(core, z, SLOTS - 1), extra_recv).start()

        def hand_extra(step, carry):
            to = lax.rem(grid + step, SIDE * SIDE)
            pltpu.make_async_remote_copy(
                src_ref=extra.at[to], dst_ref=slots(core, z, SLOTS - 1), send_sem=extra_send,
                recv_sem=extra_recv, device_id=at_grid(to), device_id_type=MESH).start()
            return carry

        lax.fori_loop(1, SIDE * SIDE, hand_extra, 0)

    def piece_of(source, piece):
        start, size = PIECES[piece]
        return slots(core, source, start, size)

    def pass_on(source, piece, to, recv_sem):
        ref = piece_of(source, piece)
        pltpu.make_async_remote_copy(
            src_ref=ref, dst_ref=ref, send_sem=z_send, recv_sem=recv_sem, device_id=to, device_id_type=MESH).start()

    def to_pair(source, piece):
        ref = piece_of(source, piece)
        pltpu.make_async_remote_copy(
            src_ref=ref, dst_ref=ref, send_sem=pair_send, recv_sem=pair_recv, device_id=pair,
            device_id_type=MESH).start()

    def await_bytes(ref, sem):
        pltpu.make_async_copy(ref, ref, sem).wait()

    for piece in range(4):
        await_bytes(slots(core, z, 4 * piece, 4), pack_recv.at[piece])
        if piece == 3:
            await_bytes(slots(core, z, SLOTS - 1), extra_recv)
        pass_on(z, piece, up, right_recv.at[1, piece])
        pass_on(z, piece, down, left_recv.at[1, piece])
        to_pair(z, piece)

    def leaf_of(k):
        found, index = 0, 0
        for t in range(NS2):
            same = (leaf[0, t] == k).astype(jnp.int32)
            found = found + same
            index = index + same * t
        return jnp.minimum(index, NS2 - 1), found.astype(F32)

    def factors():
        for load in loads:
            load.wait()
        minv_s = split(minv[...])
        linv_s = split(linv[...])
        v0_s = split(product(split(first_raw[...]), linv_s))
        v0_hi[...], v0_lo[...] = v0_s
        for part in range(2):
            vblocks[part] = product(split(loff[part].reshape(NS2 * SUB, BS)), linv_s).reshape(NS2, SUB, BS)
        square = product_t(minv_s, minv_s)
        base[0] = square
        turned = product(split(square), v0_s)
        base[1] = -turned
        base[2] = product_t(linv_s, linv_s) + product_t(v0_s, split(turned))
        for part in range(2):
            def rows(q, carry):
                raw = moff[part, pl.ds(q * 4, 4)].reshape(BS, BS)
                u = product(split(raw), (split(minv[...])))
                u_s = split(u)
                uv = product(u_s, (v0_hi[...], v0_lo[...]))
                spread = []
                for j in range(4):
                    index, mark = leaf_of(q * 4 + j)
                    spread.append(vblocks[part, index] * mark)
                t = jnp.concatenate(spread, axis=0) - uv
                t_s = split(t)
                at = pl.ds(pl.multiple_of(q * BS, BS), BS)
                for kind, pieces in ((0, u_s), (1, t_s)):
                    w_hi[part, at, kind * BS:(kind + 1) * BS] = pieces[0]
                    w_lo[part, at, kind * BS:(kind + 1) * BS] = pieces[1]
                if part == 1:
                    for kind, value in ((0, u), (1, t)):
                        high, low = split(value.T)
                        wt_hi[kind * BS:(kind + 1) * BS, at] = high
                        wt_lo[kind * BS:(kind + 1) * BS, at] = low
                return carry
            lax.fori_loop(0, 3, rows, 0)

    factors()

    for step in range(1, 5):
        below = lax.rem(z + RING - step, RING)
        above = lax.rem(z + step, RING)
        for piece in range(4):
            if step < 4 or piece < 2:
                await_bytes(piece_of(below, piece), right_recv.at[step, piece])
                if step < 3 or (step == 3 and piece < 2):
                    pass_on(below, piece, up, right_recv.at[step + 1, piece])
                to_pair(below, piece)
            if step < 4 or piece >= 2:
                await_bytes(piece_of(above, piece), left_recv.at[step, piece])
                if step < 3 or (step == 3 and piece >= 2):
                    pass_on(above, piece, down, left_recv.at[step + 1, piece])
                to_pair(above, piece)
    await_bytes(slots(1 - core, 0, 0, RING * SLOTS), pair_recv)

    narrow = lax.broadcasted_iota(jnp.int32, (SUB, 128), 1) < SUB

    def select(k, carry):
        si = struct[0, k]
        gi, ai = si >> 1, si & 1
        row = pl.ds(pl.multiple_of(k * SUB, SUB), SUB)
        for p in range(NS1 // 2):
            sides = []
            for h in range(2):
                sj = struct[0, 2 * p + h]
                bj, cj = sj >> 1, sj & 1
                beyond = (gi > bj).astype(jnp.int32)
                plain = (cj == (ai ^ beyond)).astype(jnp.int32)
                own = ((gi == bj).astype(jnp.int32)) * (1 - ai) * cj
                slot = own * (SLOTS - 1) + (1 - own) * gi
                there = (1 - own) * ai
                weight = (plain + own).astype(F32) * (1.0 - 0.5 * (si == sj).astype(F32))
                stay = (there == h).astype(F32)
                share = gathered[((bj & 1) * RING + (bj >> 1)) * SLOTS + slot]
                sides.append(share * (weight * stay) + pltpu.roll(share, SUB, 1) * (weight * (1.0 - stay)))
            high, low = split(jnp.where(narrow, sides[0], sides[1]))
            a_hi[row, p * 128:(p + 1) * 128] = high
            a_lo[row, p * 128:(p + 1) * 128] = low
        return carry

    lax.fori_loop(0, NS1, select, 0)

    def send(src, dst, send_sem, recv_sem, to):
        copy = pltpu.make_async_remote_copy(
            src_ref=src, dst_ref=dst, send_sem=send_sem, recv_sem=recv_sem, device_id=to, device_id_type=MESH)
        copy.start()
        return copy

    started = []

    def first_hop(axis, chunk, half, recv, sends, recvs):
        me = place[axis]
        plus, minus = around[axis]
        far, nxt, prv = lax.rem(me + 2, SIDE), lax.rem(me + 1, SIDE), lax.rem(me + 3, SIDE)
        started.append(send(chunk(far, 0), recv.at[0], sends.at[0], recvs.at[0], plus))
        started.append(send(chunk(far, 1), recv.at[2], sends.at[2], recvs.at[2], minus))
        started.append(send(chunk(nxt, 1), recv.at[1], sends.at[1], recvs.at[1], plus))
        started.append(send(chunk(prv, 0), recv.at[3], sends.at[3], recvs.at[3], minus))

    def second_hop(axis, chunk, half, recv, comb, sends, recvs):
        me = place[axis]
        plus, minus = around[axis]
        nxt, prv = lax.rem(me + 1, SIDE), lax.rem(me + 3, SIDE)
        await_bytes(recv.at[0], recvs.at[0])
        comb[0] = recv[0] + chunk(nxt, 0)[...]
        started.append(send(comb.at[0], recv.at[4], sends.at[4], recvs.at[4], plus))
        await_bytes(recv.at[2], recvs.at[2])
        comb[1] = recv[2] + chunk(prv, 1)[...]
        started.append(send(comb.at[1], recv.at[5], sends.at[5], recvs.at[5], minus))

    def arrive(recv, recvs):
        for slot in (1, 3, 4, 5):
            await_bytes(recv.at[slot], recvs.at[slot])

    def left_rows(r, carry):
        at = pl.ds(pl.multiple_of(r * BS, BS), BS)
        ysum[0, pl.ds(r * 4, 4)] = product((a_hi[at, :], a_lo[at, :]), (w_hi[0], w_lo[0])).reshape(4, SUB, 2 * BS)
        return carry

    lax.fori_loop(0, 3, left_rows, 0)

    def gram(left, right):
        at = slice(left * BS, (left + 1) * BS)
        return product((wt_hi[at, :], wt_lo[at, :]), split(ysum[0, :, :, right * BS:(right + 1) * BS].reshape(ROWS, BS)))

    def put_gram(index, value):
        for part in range(16):
            if part * 48 // BS > index or (part * 48 + 47) // BS < index:
                continue
            low, high = max(part * 48, index * BS), min(part * 48 + 48, index * BS + BS)
            gsend[part // 8, part % 8 // 2, part % 2, low - part * 48:high - part * 48, :] = (
                value[low - index * BS:high - index * BS, :])

    h00 = gram(0, 0)
    put_gram(0, h00 + h00.T)
    put_gram(1, gram(0, 1) + gram(1, 0).T)
    h11 = gram(1, 1)
    put_gram(2, h11 + h11.T)

    def g_chunk(axis):
        return lambda t, h: gsend.at[axis, t, h]

    def y_chunk(axis):
        return lambda t, h: ysend.at[axis, t, h]

    for axis in (0, 1):
        first_hop(axis, g_chunk(axis), 48, grecv.at[axis], g_send_sem.at[axis], g_recv_sem.at[axis])

    def pack_rows(source, axis):
        for n in range(OUTS):
            if n < NS1:
                value = ysum[source, n, :, 0:BS]
            else:
                value = ysum[source, leaf[0, n - NS1], :, BS:2 * BS]
            for t in range(SIDE):
                ysend[axis, t, n // 9, n % 9] = value[t * SLICE:(t + 1) * SLICE, :]

    pack_rows(0, 1)
    first_hop(1, y_chunk(1), 9, yrecv.at[1], y_send_sem.at[1], y_recv_sem.at[1])

    for axis in (0, 1):
        second_hop(axis, g_chunk(axis), 48, grecv.at[axis], gcomb.at[axis], g_send_sem.at[axis], g_recv_sem.at[axis])

    def right_rows(r, carry):
        at = pl.ds(pl.multiple_of(r * BS, BS), BS)
        ysum[1, pl.ds(r * 4, 4)] = product_t((a_hi[:, at], a_lo[:, at]), (w_hi[1], w_lo[1])).reshape(4, SUB, 2 * BS)
        return carry

    lax.fori_loop(0, 3, right_rows, 0)

    def g_sum_and_exchange(axis):
        recv, recvs, sends = grecv.at[axis], g_recv_sem.at[axis], g_send_sem.at[axis]
        me = place[axis]
        arrive(recv, recvs)
        gred[axis, 0] = (gsend[axis, me, 0] + recv[3]) + recv[4]
        gred[axis, 1] = (gsend[axis, me, 1] + recv[1]) + recv[5]
        plus, minus = around[1 - axis]
        started.append(send(gred.at[axis], gexch.at[axis, 0], sends.at[6], recvs.at[6], plus))
        started.append(send(gred.at[axis], gexch.at[axis, 1], sends.at[7], recvs.at[7], minus))

    def g_exchange_on(axis):
        recvs, sends = g_recv_sem.at[axis], g_send_sem.at[axis]
        plus, minus = around[1 - axis]
        await_bytes(gexch.at[axis, 0], recvs.at[6])
        started.append(send(gexch.at[axis, 0, 0], gexch.at[axis, 2, 0], sends.at[8], recvs.at[8], plus))
        await_bytes(gexch.at[axis, 1], recvs.at[7])
        started.append(send(gexch.at[axis, 1, 1], gexch.at[axis, 2, 1], sends.at[9], recvs.at[9], minus))

    def g_spread(axis):
        recvs, sends = g_recv_sem.at[axis], g_send_sem.at[axis]
        me = place[axis]
        plus, minus = around[axis]
        await_bytes(gexch.at[axis, 2, 0], recvs.at[8])
        await_bytes(gexch.at[axis, 2, 1], recvs.at[9])
        gall[axis, me] = (gred[axis] + gexch[axis, 2]) + (gexch[axis, 0] + gexch[axis, 1])
        started.append(send(gall.at[axis, me], gall.at[axis, me], sends.at[10], recvs.at[10], plus))
        started.append(send(gall.at[axis, me], gall.at[axis, me], sends.at[11], recvs.at[11], minus))

    def g_spread_on(axis):
        recvs, sends = g_recv_sem.at[axis], g_send_sem.at[axis]
        me = place[axis]
        plus, minus = around[axis]
        prv, nxt, far = lax.rem(me + 3, SIDE), lax.rem(me + 1, SIDE), lax.rem(me + 2, SIDE)
        await_bytes(gall.at[axis, prv], recvs.at[10])
        started.append(send(gall.at[axis, prv, 0], gall.at[axis, prv, 0], sends.at[12], recvs.at[12], plus))
        await_bytes(gall.at[axis, nxt], recvs.at[11])
        started.append(send(gall.at[axis, nxt, 1], gall.at[axis, nxt, 1], sends.at[13], recvs.at[13], minus))

    for axis in (0, 1):
        g_sum_and_exchange(axis)
    pack_rows(1, 0)
    first_hop(0, y_chunk(0), 9, yrecv.at[0], y_send_sem.at[0], y_recv_sem.at[0])
    for axis in (0, 1):
        g_exchange_on(axis)
    second_hop(1, y_chunk(1), 9, yrecv.at[1], ycomb.at[1], y_send_sem.at[1], y_recv_sem.at[1])
    for axis in (0, 1):
        g_spread(axis)
    second_hop(0, y_chunk(0), 9, yrecv.at[0], ycomb.at[0], y_send_sem.at[0], y_recv_sem.at[0])
    for axis in (0, 1):
        g_spread_on(axis)

    for axis in (1, 0):
        arrive(yrecv.at[axis], y_recv_sem.at[axis])
    for half, direct, through in ((0, 3, 4), (1, 1, 5)):
        total = 0.0
        for axis in (0, 1):
            total = total + ((ysend[axis, place[axis], half] + yrecv[axis, direct]) + yrecv[axis, through])
        ycomb[2, half] = -total
    for n in range(NS1):
        mid_out[n] = ycomb[2, n // 9, n % 9]
        index, mark = leaf_of(n)
        leaf_out[n] = ycomb[2, 1, index + (NS1 - 9)] * mark

    for axis in (0, 1):
        far = lax.rem(place[axis] + 2, SIDE)
        await_bytes(gall.at[axis, far, 0], g_recv_sem.at[axis, 12])
        await_bytes(gall.at[axis, far, 1], g_recv_sem.at[axis, 13])
    total = gall[...].reshape(3 * BS, BS)
    diag_out[...] = total[0:BS] + base[0]
    parent_out[...] = total[BS:2 * BS] + base[1]
    leaf_diag_out[...] = total[2 * BS:3 * BS] + base[2]

    for copy in started:
        copy.wait_send()
    await_bytes(packed.at[pl.ds(0, SIDE * SIDE - 1)], pack_send)

    @pl.when(grid == branch)
    def _():
        await_bytes(extra.at[pl.ds(0, SIDE * SIDE - 1)], extra_send)

    await_bytes(slots(core, 0, 0, (RING - 1) * SLOTS), z_send)
    await_bytes(slots(core, 0, 0, RING * SLOTS), pair_send)


def on_device(sigma_top, mid_struct, leaf_struct, mid_inv, mid_off, leaf_inv, leaf_off):
    smem = pl.BlockSpec(memory_space=pltpu.SMEM)
    vmem = pl.BlockSpec(memory_space=pltpu.VMEM)
    hbm = pl.BlockSpec(memory_space=pl.ANY)
    dma = pltpu.SemaphoreType.DMA
    outs = pl.pallas_call(
        kernel,
        out_shape=(
            jax.ShapeDtypeStruct((NS1, SLICE, BS), F32),
            jax.ShapeDtypeStruct((BS, BS), F32),
            jax.ShapeDtypeStruct((NS1, SLICE, BS), F32),
            jax.ShapeDtypeStruct((BS, BS), F32),
            jax.ShapeDtypeStruct((BS, BS), F32),
        ),
        in_specs=[smem, smem, vmem, hbm, hbm, hbm, hbm],
        out_specs=(vmem,) * 5,
        scratch_shapes=[
            pltpu.VMEM((SIDE * SIDE, SUB, 128), F32),
            pltpu.VMEM((SIDE * SIDE, SUB, 128), F32),
            pltpu.VMEM((2 * RING * SLOTS, SUB, 128), F32),
            pltpu.VMEM((2, NS1, SUB, BS), F32),
            pltpu.VMEM((2, NS2, SUB, BS), F32),
            pltpu.VMEM((BS, BS), F32),
            pltpu.VMEM((BS, BS), F32),
            pltpu.VMEM((BS, BS), F32),
            pltpu.VMEM((2, NS2, SUB, BS), F32),
            pltpu.VMEM((BS, BS), BF16),
            pltpu.VMEM((BS, BS), BF16),
            pltpu.VMEM((3, BS, BS), F32),
            pltpu.VMEM((2, ROWS, 2 * BS), BF16),
            pltpu.VMEM((2, ROWS, 2 * BS), BF16),
            pltpu.VMEM((2 * BS, ROWS), BF16),
            pltpu.VMEM((2 * BS, ROWS), BF16),
            pltpu.VMEM((ROWS, ROWS), BF16),
            pltpu.VMEM((ROWS, ROWS), BF16),
            pltpu.VMEM((2, NS1, SUB, 2 * BS), F32),
            pltpu.VMEM((2, SIDE, 2, 9, SLICE, BS), F32),
            pltpu.VMEM((2, 6, 9, SLICE, BS), F32),
            pltpu.VMEM((3, 2, 9, SLICE, BS), F32),
            pltpu.VMEM((2, SIDE, 2, 48, BS), F32),
            pltpu.VMEM((2, 6, 48, BS), F32),
            pltpu.VMEM((2, 2, 48, BS), F32),
            pltpu.VMEM((2, 2, 48, BS), F32),
            pltpu.VMEM((2, 3, 2, 48, BS), F32),
            pltpu.VMEM((2, SIDE, 2, 48, BS), F32),
            dma((13,)),
            dma,
            dma((4,)),
            dma,
            dma,
            dma,
            dma((5, 4)),
            dma((5, 4)),
            dma,
            dma,
            dma((2, 6)),
            dma((2, 6)),
            dma((2, 14)),
            dma((2, 14)),
        ],
        compiler_params=pltpu.CompilerParams(
            collective_id=0, has_side_effects=True, vmem_limit_bytes=52 * 1024 * 1024),
    )(mid_struct, leaf_struct, sigma_top, mid_inv, mid_off, leaf_inv, leaf_off)
    return tuple(out[None] for out in outs)


def solution(mesh):
    in_specs = (
        P("grid", "branch"),
        P("branch", None),
        P("branch", None),
        P("branch", None, None),
        P("branch", None, None, None),
        P("branch", None, None),
        P("branch", None, None, None),
    )
    out_specs = (
        P("branch", None, "grid", None),
        P("branch", None, None),
        P("branch", None, "grid", None),
        P("branch", None, None),
        P("branch", None, None),
    )
    return jax.shard_map(
        on_device, mesh=mesh, in_specs=in_specs, out_specs=out_specs, check_vma=False
    )
```

time: 410 us -> 111 us (0.27)
  waiting for transfers between devices: 192 us -> 0 us
  Pallas kernels: 0 us -> 104 us
  matrix products: 75.8 us -> 0 us
  other arithmetic: 46.6 us -> 0 us
  loops' own time: 45.2 us -> 0 us
  local copies, waits for them, and re-layouts: 34.5 us -> 6.66 us
  between operations: 14.2 us -> 0.66 us
    psum x1 -> x0, waiting for transfers between devices: 128 us -> none  [on_device(): summed = lax.psum(chosen, 'grid')]
    pallas_call x0 -> x1, Pallas kernels: none -> 104 us  [on_device(): pl.pallas_call(kernel, out_shape=(jax.ShapeDtypeStruct((NS1, SLICE, BS),...]
    dot_general x24 -> x0, matrix products: 75.8 us -> none  [the longest x12 35 us: add_left(): lax.dot_general(column, weights, (((0,), (0,)), ((), ())), precision=high...]
    all_gather x1 -> x0, waiting for transfers between devices: 62.8 us -> none  [on_device(): lax.all_gather(sigma_top, 'branch', axis=1, tiled=True)]
    another operation x33 -> x0, loops' own time: 45.2 us -> none  [the longest x32 23.8 us: step(): lax.cond(found, lambda inner: add_block(inner, column, where), lambda inn...]
    another operation x32 -> x0, other arithmetic: 20.9 us -> none  [step(): where = jnp.argmax(match.astype(jnp.int32))]
    reduce_or x32 -> x0, other arithmetic: 20.2 us -> none  [step(): found = jnp.any(match)]
    dynamic_slice x12 -> x0, local copies, waits for them, and re-layouts: 13 us -> none  [add_left(): current = lax.dynamic_index_in_dim(acc, where, 0, keepdims=False)]
  transfers between devices with their start and end apart: 2 -> 0, of which waited for: 2 -> 0; matrix products, arithmetic and copies ran while one was open for 9% -> 0% of each run, Pallas kernels for 0% -> 0%
where the time goes in v1:
time: 111 us
  Pallas kernels  104 us (94%)
  local copies, waits for them, and re-layouts  6.66 us (6%)
    pallas_call x1, Pallas kernels, on_device(): pl.pallas_call(kernel, out_shape=(jax.ShapeDtypeStruct((NS1, SLICE, BS),...  104 us
    unnamed x13, local copies, waits for them, and re-layouts  6.66 us

profile of v1, /device:TPU:1, one launch (start us, length us, event | category | flops | bytes accessed | tf_op | source)
XLA Modules:
  0.0 111.2 jit_solution(4467979309209977092)
XLA Ops:
  0.6 0.0 copy-start
  0.6 0.9 copy-done
  1.6 0.0 copy-start.1
  1.6 0.9 copy-done.1
  2.5 0.0 copy-start.2
  2.5 0.7 copy-done.2
  3.2 0.0 copy-start.3
  3.2 0.7 copy-done.3
  3.8 103.9 %shard_map.110 = (f32[12,16,256]{2,1,0:T(8,128)S(1)}, f32[256,256]{1,0:T(8,128)S(1)}, f32[12,16,256]{2,1,0:T(8,128)S(1)}, f32[256,256]{1,0:T(8,128)S(1)}, f32[256,256]{1,0:T(8,128)S(1)}) custom-call(s32[1,12]{1,0:T(1,128)S(1)} %copy-done.2, s32[1,6]{1,0:T(1,128)S(1)} %copy-done.3, f32[512,512]{1,0:T(8,128)} %sigma.1, f32[1,256,256]{2,1,0:T(8,128)S(1)} %copy-done, ...), custom_call_target="tpu_custom_call" | custom-call | tf_op jit(solution)/shard_map/pallas_call | solution.py:445
  107.7 0.7 copy.17
  108.4 0.7 copy.18
  109.1 0.7 copy.19
  109.8 0.7 copy.20
  110.5 0.7 copy.21
Async XLA Ops:
  0.6 1.0 copy-start
  1.6 0.9 copy-start.1
  2.5 0.7 copy-start.2
  3.2 0.7 copy-start.3

commit v2 on v1

--- a/solution.py
+++ b/solution.py
@@ -1,5 +1,3 @@
-import functools
-
 import jax
 import jax.numpy as jnp
 from jax import lax
@@ -18,7 +16,8 @@
 SUB = BS // SIDE
 SLICE = 16
 SLOTS = 17
-PIECES = ((0, 4), (4, 4), (8, 4), (12, 5))
+HALF = SUB // 2
+PIECES = ((0, 0, 8), (0, 8, 9), (1, 0, 8), (1, 8, 9))
 ROWS = NS1 * SUB
 OUTS = NS1 + NS2
 
@@ -39,10 +38,11 @@
 
 
 def kernel(
-    struct, leaf, sigma, minv_hbm, moff_hbm, linv_hbm, loff_hbm,
-    mid_out, diag_out, leaf_out, parent_out, leaf_diag_out,
-    packed, extra, gathered, moff, loff, first_raw, minv, linv, vblocks, v0_hi, v0_lo, base,
+    struct_hbm, leaf_hbm, sigma_hbm, minv_hbm, moff_hbm, linv_hbm, loff_hbm,
+    mid_hbm, column_hbm, gram_hbm,
+    struct, leaf, sigma, packed, extra, gathered, moff, loff, first_raw, minv, linv, vblocks, v0_hi, v0_lo, base,
     w_hi, w_lo, wt_hi, wt_lo, a_hi, a_lo, ysum, ysend, yrecv, ycomb, gsend, grecv, gcomb, gred, gexch, gall,
+    column_out, gram_out, out_sem,
     load_sem, pack_send, pack_recv, extra_send, extra_recv, z_send, right_recv, left_recv,
     pair_send, pair_recv, y_send_sem, y_recv_sem, g_send_sem, g_recv_sem,
 ):
@@ -51,8 +51,8 @@
     z, core = branch // 2, branch % 2
     y, x = grid // SIDE, grid % SIDE
 
-    def slots(which_core, source, slot, size=None):
-        start = (which_core * RING + source) * SLOTS + slot
+    def slots(which_core, source, half, slot, size=None):
+        start = ((which_core * RING + source) * 2 + half) * SLOTS + slot
         return gathered.at[start] if size is None else gathered.at[pl.ds(start, size)]
 
     def at_grid(index):
@@ -85,8 +85,10 @@
             moff_hbm.at[0, :, pl.ds(row_r, SLICE), :], moff.at[1, :, into, :], load_sem.at[5 + m]))
         loads.append(pltpu.make_async_copy(
             loff_hbm.at[0, pl.ds(1, NS2), pl.ds(row_r, SLICE), :], loff.at[1, :, into, :], load_sem.at[9 + m]))
-    for load in loads:
-        load.start()
+    loads.append(pltpu.make_async_copy(struct_hbm, struct, load_sem.at[13]))
+    loads.append(pltpu.make_async_copy(leaf_hbm, leaf, load_sem.at[14]))
+    own = pltpu.make_async_copy(sigma_hbm, sigma, load_sem.at[15])
+    own.start()
 
     barrier = pltpu.get_barrier_semaphore()
 
@@ -98,6 +100,10 @@
     lax.fori_loop(1, SIDE * SIDE, greet, 0)
     for other in (up, down, pair):
         pl.semaphore_signal(barrier, inc=1, device_id=other, device_id_type=MESH)
+
+    for load in loads:
+        load.start()
+    own.wait()
 
     flip = (grid > branch).astype(jnp.int32)
     lane = lax.broadcasted_iota(jnp.int32, (BS, 128), 1)
@@ -110,7 +116,7 @@
             for m in range(SIDE):
                 for xx in range(SIDE):
                     start = m * SUB + xx * SLICE
-                    packed[side * SIDE + xx, m * SLICE:(m + 1) * SLICE, :] = value[start:start + SLICE, :]
+                    packed[m // 2, side * SIDE + xx, m % 2 * SLICE:(m % 2 + 1) * SLICE, :] = value[start:start + SLICE, :]
 
     @pl.when(grid == branch)
     def _():
@@ -120,37 +126,39 @@
                 for m in range(SIDE):
                     for xx in range(SIDE):
                         start = m * SUB + xx * SLICE
-                        extra[side * SIDE + xx, m * SLICE:(m + 1) * SLICE, :] = turned[start:start + SLICE, :]
+                        extra[m // 2, side * SIDE + xx, m % 2 * SLICE:(m % 2 + 1) * SLICE, :] = turned[start:start + SLICE, :]
 
     pl.semaphore_wait(barrier, SIDE * SIDE + 2)
 
-    pltpu.make_async_copy(packed.at[grid], slots(core, z, grid), pack_recv.at[grid // SIDE]).start()
-
-    def hand_out(step, carry):
-        to = lax.rem(grid + step, SIDE * SIDE)
-        pltpu.make_async_remote_copy(
-            src_ref=packed.at[to], dst_ref=slots(core, z, grid), send_sem=pack_send,
-            recv_sem=pack_recv.at[grid // SIDE], device_id=at_grid(to), device_id_type=MESH).start()
-        return carry
-
-    lax.fori_loop(1, SIDE * SIDE, hand_out, 0)
-
-    @pl.when(grid == branch)
-    def _():
-        pltpu.make_async_copy(extra.at[grid], slots(core, z, SLOTS - 1), extra_recv).start()
-
-        def hand_extra(step, carry):
+    for half in range(2):
+        pltpu.make_async_copy(packed.at[half, grid], slots(core, z, half, grid), pack_recv.at[half]).start()
+
+        def hand_out(step, carry):
             to = lax.rem(grid + step, SIDE * SIDE)
             pltpu.make_async_remote_copy(
-                src_ref=extra.at[to], dst_ref=slots(core, z, SLOTS - 1), send_sem=extra_send,
-                recv_sem=extra_recv, device_id=at_grid(to), device_id_type=MESH).start()
+                src_ref=packed.at[half, to], dst_ref=slots(core, z, half, grid), send_sem=pack_send,
+                recv_sem=pack_recv.at[half], device_id=at_grid(to), device_id_type=MESH).start()
             return carry
 
-        lax.fori_loop(1, SIDE * SIDE, hand_extra, 0)
+        lax.fori_loop(1, SIDE * SIDE, hand_out, 0)
+
+        @pl.when(grid == branch)
+        def _():
+            own_slot = slots(core, z, half, SLOTS - 1)
+            pltpu.make_async_copy(extra.at[half, grid], own_slot, extra_recv.at[half]).start()
+
+            def hand_extra(step, carry):
+                to = lax.rem(grid + step, SIDE * SIDE)
+                pltpu.make_async_remote_copy(
+                    src_ref=extra.at[half, to], dst_ref=own_slot, send_sem=extra_send,
+                    recv_sem=extra_recv.at[half], device_id=at_grid(to), device_id_type=MESH).start()
+                return carry
+
+            lax.fori_loop(1, SIDE * SIDE, hand_extra, 0)
 
     def piece_of(source, piece):
-        start, size = PIECES[piece]
-        return slots(core, source, start, size)
+        half, start, size = PIECES[piece]
+        return slots(core, source, half, start, size)
 
     def pass_on(source, piece, to, recv_sem):
         ref = piece_of(source, piece)
@@ -167,9 +175,10 @@
         pltpu.make_async_copy(ref, ref, sem).wait()
 
     for piece in range(4):
-        await_bytes(slots(core, z, 4 * piece, 4), pack_recv.at[piece])
-        if piece == 3:
-            await_bytes(slots(core, z, SLOTS - 1), extra_recv)
+        half = PIECES[piece][0]
+        if piece % 2 == 0:
+            await_bytes(slots(core, z, half, 0, SIDE * SIDE), pack_recv.at[half])
+            await_bytes(slots(core, z, half, SLOTS - 1), extra_recv.at[half])
         pass_on(z, piece, up, right_recv.at[1, piece])
         pass_on(z, piece, down, left_recv.at[1, piece])
         to_pair(z, piece)
@@ -236,16 +245,15 @@
                 if step < 3 or (step == 3 and piece >= 2):
                     pass_on(above, piece, down, left_recv.at[step + 1, piece])
                 to_pair(above, piece)
-    await_bytes(slots(1 - core, 0, 0, RING * SLOTS), pair_recv)
-
-    narrow = lax.broadcasted_iota(jnp.int32, (SUB, 128), 1) < SUB
+    await_bytes(slots(1 - core, 0, 0, 0, 2 * RING * SLOTS), pair_recv)
+
+    narrow = lax.broadcasted_iota(jnp.int32, (HALF, 128), 1) < SUB
 
     def select(k, carry):
         si = struct[0, k]
         gi, ai = si >> 1, si & 1
-        row = pl.ds(pl.multiple_of(k * SUB, SUB), SUB)
         for p in range(NS1 // 2):
-            sides = []
+            sides = [[], []]
             for h in range(2):
                 sj = struct[0, 2 * p + h]
                 bj, cj = sj >> 1, sj & 1
@@ -256,11 +264,15 @@
                 there = (1 - own) * ai
                 weight = (plain + own).astype(F32) * (1.0 - 0.5 * (si == sj).astype(F32))
                 stay = (there == h).astype(F32)
-                share = gathered[((bj & 1) * RING + (bj >> 1)) * SLOTS + slot]
-                sides.append(share * (weight * stay) + pltpu.roll(share, SUB, 1) * (weight * (1.0 - stay)))
-            high, low = split(jnp.where(narrow, sides[0], sides[1]))
-            a_hi[row, p * 128:(p + 1) * 128] = high
-            a_lo[row, p * 128:(p + 1) * 128] = low
+                for half in range(2):
+                    share = gathered[(((bj & 1) * RING + (bj >> 1)) * 2 + half) * SLOTS + slot]
+                    sides[half].append(
+                        share * (weight * stay) + pltpu.roll(share, SUB, 1) * (weight * (1.0 - stay)))
+            for half in range(2):
+                row = pl.ds(pl.multiple_of(k * SUB + half * HALF, HALF), HALF)
+                high, low = split(jnp.where(narrow, sides[half][0], sides[half][1]))
+                a_hi[row, p * 128:(p + 1) * 128] = high
+                a_lo[row, p * 128:(p + 1) * 128] = low
         return carry
 
     lax.fori_loop(0, NS1, select, 0)
@@ -273,16 +285,19 @@
 
     started = []
 
-    def first_hop(axis, chunk, half, recv, sends, recvs):
-        me = place[axis]
+    def first_hop(axis, chunk, recv, sends, recvs):
         plus, minus = around[axis]
-        far, nxt, prv = lax.rem(me + 2, SIDE), lax.rem(me + 1, SIDE), lax.rem(me + 3, SIDE)
+        far = lax.rem(place[axis] + 2, SIDE)
         started.append(send(chunk(far, 0), recv.at[0], sends.at[0], recvs.at[0], plus))
         started.append(send(chunk(far, 1), recv.at[2], sends.at[2], recvs.at[2], minus))
+
+    def direct_hop(axis, chunk, recv, sends, recvs):
+        plus, minus = around[axis]
+        nxt, prv = lax.rem(place[axis] + 1, SIDE), lax.rem(place[axis] + 3, SIDE)
         started.append(send(chunk(nxt, 1), recv.at[1], sends.at[1], recvs.at[1], plus))
         started.append(send(chunk(prv, 0), recv.at[3], sends.at[3], recvs.at[3], minus))
 
-    def second_hop(axis, chunk, half, recv, comb, sends, recvs):
+    def second_hop(axis, chunk, recv, comb, sends, recvs):
         me = place[axis]
         plus, minus = around[axis]
         nxt, prv = lax.rem(me + 1, SIDE), lax.rem(me + 3, SIDE)
@@ -302,8 +317,6 @@
         ysum[0, pl.ds(r * 4, 4)] = product((a_hi[at, :], a_lo[at, :]), (w_hi[0], w_lo[0])).reshape(4, SUB, 2 * BS)
         return carry
 
-    lax.fori_loop(0, 3, left_rows, 0)
-
     def gram(left, right):
         at = slice(left * BS, (left + 1) * BS)
         return product((wt_hi[at, :], wt_lo[at, :]), split(ysum[0, :, :, right * BS:(right + 1) * BS].reshape(ROWS, BS)))
@@ -316,20 +329,17 @@
             gsend[part // 8, part % 8 // 2, part % 2, low - part * 48:high - part * 48, :] = (
                 value[low - index * BS:high - index * BS, :])
 
-    h00 = gram(0, 0)
-    put_gram(0, h00 + h00.T)
-    put_gram(1, gram(0, 1) + gram(1, 0).T)
-    h11 = gram(1, 1)
-    put_gram(2, h11 + h11.T)
-
     def g_chunk(axis):
         return lambda t, h: gsend.at[axis, t, h]
 
     def y_chunk(axis):
         return lambda t, h: ysend.at[axis, t, h]
 
-    for axis in (0, 1):
-        first_hop(axis, g_chunk(axis), 48, grecv.at[axis], g_send_sem.at[axis], g_recv_sem.at[axis])
+    def g_ring(axis):
+        return axis, g_chunk(axis), grecv.at[axis], g_send_sem.at[axis], g_recv_sem.at[axis]
+
+    def y_ring(axis):
+        return axis, y_chunk(axis), yrecv.at[axis], y_send_sem.at[axis], y_recv_sem.at[axis]
 
     def pack_rows(source, axis):
         for n in range(OUTS):
@@ -340,18 +350,11 @@
             for t in range(SIDE):
                 ysend[axis, t, n // 9, n % 9] = value[t * SLICE:(t + 1) * SLICE, :]
 
-    pack_rows(0, 1)
-    first_hop(1, y_chunk(1), 9, yrecv.at[1], y_send_sem.at[1], y_recv_sem.at[1])
-
-    for axis in (0, 1):
-        second_hop(axis, g_chunk(axis), 48, grecv.at[axis], gcomb.at[axis], g_send_sem.at[axis], g_recv_sem.at[axis])
-
     def right_rows(r, carry):
         at = pl.ds(pl.multiple_of(r * BS, BS), BS)
         ysum[1, pl.ds(r * 4, 4)] = product_t((a_hi[:, at], a_lo[:, at]), (w_hi[1], w_lo[1])).reshape(4, SUB, 2 * BS)
         return carry
 
-    lax.fori_loop(0, 3, right_rows, 0)
 
     def g_sum_and_exchange(axis):
         recv, recvs, sends = grecv.at[axis], g_recv_sem.at[axis], g_send_sem.at[axis]
@@ -391,16 +394,38 @@
         await_bytes(gall.at[axis, nxt], recvs.at[11])
         started.append(send(gall.at[axis, nxt, 1], gall.at[axis, nxt, 1], sends.at[13], recvs.at[13], minus))
 
+    def g_second(axis):
+        second_hop(axis, g_chunk(axis), grecv.at[axis], gcomb.at[axis], g_send_sem.at[axis], g_recv_sem.at[axis])
+
+    def y_second(axis):
+        second_hop(axis, y_chunk(axis), yrecv.at[axis], ycomb.at[axis], y_send_sem.at[axis], y_recv_sem.at[axis])
+
+    lax.fori_loop(0, 3, left_rows, 0)
+    pack_rows(0, 1)
+    first_hop(*y_ring(1))
+    h00 = gram(0, 0)
+    put_gram(0, h00 + h00.T)
+    put_gram(1, gram(0, 1) + gram(1, 0).T)
+    h11 = gram(1, 1)
+    put_gram(2, h11 + h11.T)
+    for axis in (0, 1):
+        first_hop(*g_ring(axis))
+        direct_hop(*g_ring(axis))
+    direct_hop(*y_ring(1))
+    lax.fori_loop(0, 3, right_rows, 0)
+    pack_rows(1, 0)
+    for axis in (0, 1):
+        g_second(axis)
+    first_hop(*y_ring(0))
+    y_second(1)
     for axis in (0, 1):
         g_sum_and_exchange(axis)
-    pack_rows(1, 0)
-    first_hop(0, y_chunk(0), 9, yrecv.at[0], y_send_sem.at[0], y_recv_sem.at[0])
+    direct_hop(*y_ring(0))
     for axis in (0, 1):
         g_exchange_on(axis)
-    second_hop(1, y_chunk(1), 9, yrecv.at[1], ycomb.at[1], y_send_sem.at[1], y_recv_sem.at[1])
+    y_second(0)
     for axis in (0, 1):
         g_spread(axis)
-    second_hop(0, y_chunk(0), 9, yrecv.at[0], ycomb.at[0], y_send_sem.at[0], y_recv_sem.at[0])
     for axis in (0, 1):
         g_spread_on(axis)
 
@@ -412,51 +437,72 @@
             total = total + ((ysend[axis, place[axis], half] + yrecv[axis, direct]) + yrecv[axis, through])
         ycomb[2, half] = -total
     for n in range(NS1):
-        mid_out[n] = ycomb[2, n // 9, n % 9]
+        column_out[0, n] = ycomb[2, n // 9, n % 9]
         index, mark = leaf_of(n)
-        leaf_out[n] = ycomb[2, 1, index + (NS1 - 9)] * mark
-
+        column_out[1, n] = ycomb[2, 1, index + (NS1 - 9)] * mark
+
+    outs = [
+        pltpu.make_async_copy(column_out.at[0], mid_hbm, out_sem.at[0]),
+        pltpu.make_async_copy(column_out.at[1], column_hbm, out_sem.at[1]),
+        pltpu.make_async_copy(gram_out, gram_hbm, out_sem.at[2]),
+    ]
+    outs[0].start()
+    outs[1].start()
     for axis in (0, 1):
         far = lax.rem(place[axis] + 2, SIDE)
         await_bytes(gall.at[axis, far, 0], g_recv_sem.at[axis, 12])
         await_bytes(gall.at[axis, far, 1], g_recv_sem.at[axis, 13])
-    total = gall[...].reshape(3 * BS, BS)
-    diag_out[...] = total[0:BS] + base[0]
-    parent_out[...] = total[BS:2 * BS] + base[1]
-    leaf_diag_out[...] = total[2 * BS:3 * BS] + base[2]
+    gram_out[...] = gall[...].reshape(3, BS, BS) + base[...]
+
+    outs[2].start()
 
     for copy in started:
         copy.wait_send()
-    await_bytes(packed.at[pl.ds(0, SIDE * SIDE - 1)], pack_send)
+    for half in range(2):
+        await_bytes(packed.at[half, pl.ds(0, SIDE * SIDE - 1)], pack_send)
 
     @pl.when(grid == branch)
     def _():
-        await_bytes(extra.at[pl.ds(0, SIDE * SIDE - 1)], extra_send)
-
-    await_bytes(slots(core, 0, 0, (RING - 1) * SLOTS), z_send)
-    await_bytes(slots(core, 0, 0, RING * SLOTS), pair_send)
+        for half in range(2):
+            await_bytes(extra.at[half, pl.ds(0, SIDE * SIDE - 1)], extra_send)
+
+    await_bytes(slots(core, 0, 0, 0, 2 * (RING - 1) * SLOTS), z_send)
+    await_bytes(slots(core, 0, 0, 0, 2 * RING * SLOTS), pair_send)
+    for copy in outs:
+        copy.wait()
+
+
+def write_out(mid, leaf, gram, mid_out, diag_out, leaf_out, parent_out, leaf_diag_out, sem):
+    copies = [
+        pltpu.make_async_copy(src, dst.at[0], sem.at[n]) for n, (src, dst) in enumerate((
+            (mid, mid_out), (leaf, leaf_out), (gram.at[0], diag_out), (gram.at[1], parent_out),
+            (gram.at[2], leaf_diag_out)))]
+    for copy in copies:
+        copy.start()
+    for copy in copies:
+        copy.wait()
 
 
 def on_device(sigma_top, mid_struct, leaf_struct, mid_inv, mid_off, leaf_inv, leaf_off):
-    smem = pl.BlockSpec(memory_space=pltpu.SMEM)
-    vmem = pl.BlockSpec(memory_space=pltpu.VMEM)
-    hbm = pl.BlockSpec(memory_space=pl.ANY)
+    hbm = pl.BlockSpec(memory_space=pltpu.HBM)
+    anywhere = pl.BlockSpec(memory_space=pl.ANY)
     dma = pltpu.SemaphoreType.DMA
-    outs = pl.pallas_call(
+    middle, leaves, grams = pl.pallas_call(
         kernel,
         out_shape=(
             jax.ShapeDtypeStruct((NS1, SLICE, BS), F32),
-            jax.ShapeDtypeStruct((BS, BS), F32),
             jax.ShapeDtypeStruct((NS1, SLICE, BS), F32),
-            jax.ShapeDtypeStruct((BS, BS), F32),
-            jax.ShapeDtypeStruct((BS, BS), F32),
+            jax.ShapeDtypeStruct((3, BS, BS), F32),
         ),
-        in_specs=[smem, smem, vmem, hbm, hbm, hbm, hbm],
-        out_specs=(vmem,) * 5,
+        in_specs=[hbm] * 7,
+        out_specs=(hbm,) * 3,
         scratch_shapes=[
-            pltpu.VMEM((SIDE * SIDE, SUB, 128), F32),
-            pltpu.VMEM((SIDE * SIDE, SUB, 128), F32),
-            pltpu.VMEM((2 * RING * SLOTS, SUB, 128), F32),
+            pltpu.SMEM((1, NS1), jnp.int32),
+            pltpu.SMEM((1, NS2), jnp.int32),
+            pltpu.VMEM((2 * BS, 2 * BS), F32),
+            pltpu.VMEM((2, SIDE * SIDE, HALF, 128), F32),
+            pltpu.VMEM((2, SIDE * SIDE, HALF, 128), F32),
+            pltpu.VMEM((4 * RING * SLOTS, HALF, 128), F32),
             pltpu.VMEM((2, NS1, SUB, BS), F32),
             pltpu.VMEM((2, NS2, SUB, BS), F32),
             pltpu.VMEM((BS, BS), F32),
@@ -482,11 +528,14 @@
             pltpu.VMEM((2, 2, 48, BS), F32),
             pltpu.VMEM((2, 3, 2, 48, BS), F32),
             pltpu.VMEM((2, SIDE, 2, 48, BS), F32),
-            dma((13,)),
+            pltpu.VMEM((2, NS1, SLICE, BS), F32),
+            pltpu.VMEM((3, BS, BS), F32),
+            dma((3,)),
+            dma((16,)),
             dma,
-            dma((4,)),
+            dma((2,)),
             dma,
-            dma,
+            dma((2,)),
             dma,
             dma((5, 4)),
             dma((5, 4)),
@@ -498,9 +547,17 @@
             dma((2, 14)),
         ],
         compiler_params=pltpu.CompilerParams(
-            collective_id=0, has_side_effects=True, vmem_limit_bytes=52 * 1024 * 1024),
+            collective_id=0, has_side_effects=True, vmem_limit_bytes=64 * 1024 * 1024),
     )(mid_struct, leaf_struct, sigma_top, mid_inv, mid_off, leaf_inv, leaf_off)
-    return tuple(out[None] for out in outs)
+    block = jax.ShapeDtypeStruct((1, BS, BS), F32)
+    column = jax.ShapeDtypeStruct((1, NS1, SLICE, BS), F32)
+    return tuple(pl.pallas_call(
+        write_out,
+        out_shape=(column, block, column, block, block),
+        in_specs=[anywhere] * 3,
+        out_specs=(anywhere,) * 5,
+        scratch_shapes=[dma((5,))],
+    )(middle, leaves, grams))
 
 
 def solution(mesh):

time: 111 us -> 135 us (1.22)
  Pallas kernels: 104 us -> 134 us
  local copies, waits for them, and re-layouts: 6.66 us -> 0 us
    pallas_call x0 -> x1, Pallas kernels: none -> 36.9 us  [on_device(): pl.pallas_call(write_out, out_shape=(column, block, column, block, block)...]
    pallas_call x1, Pallas kernels: 104 us -> 97.2 us  [on_device(): pl.pallas_call(kernel, out_shape=(jax.ShapeDtypeStruct((NS1, SLICE, BS),...]
    unnamed x13 -> x0, local copies, waits for them, and re-layouts: 6.66 us -> none
where the time goes in v2:
time: 135 us
  Pallas kernels  134 us (99%)
    pallas_call x1, Pallas kernels, on_device(): pl.pallas_call(kernel, out_shape=(jax.ShapeDtypeStruct((NS1, SLICE, BS),...  97.2 us
    pallas_call x1, Pallas kernels, on_device(): pl.pallas_call(write_out, out_shape=(column, block, column, block, block)...  36.9 us

profile of v2, /device:TPU:1, one launch (start us, length us, event | category | flops | bytes accessed | tf_op | source)
XLA Modules:
  0.0 134.7 jit_solution(5902622490087063378)
XLA Ops:
  0.6 97.2 %shard_map.110 = (f32[12,16,256]{2,1,0:T(8,128)}, f32[12,16,256]{2,1,0:T(8,128)}, f32[3,256,256]{2,1,0:T(8,128)}) custom-call(s32[1,12]{1,0:T(1,128)} %struct_hbm.1, s32[1,6]{1,0:T(1,128)} %leaf_hbm.1, f32[512,512]{1,0:T(8,128)} %sigma_hbm.1, f32[1,256,256]{2,1,0:T(8,128)} %minv_hbm.1, f32[1,12,256,256]{3,2,1,0:T(8,128)} %moff_hbm.1, ...), custom_call_target="tpu_custom_call" | custom-call | tf_op jit(solution)/shard_map/pallas_call | solution.py:490
  97.8 36.9 %shard_map.111 = (f32[1,12,16,256]{3,2,1,0:T(8,128)}, f32[1,256,256]{2,1,0:T(8,128)}, f32[1,12,16,256]{3,2,1,0:T(8,128)}, f32[1,256,256]{2,1,0:T(8,128)}, f32[1,256,256]{2,1,0:T(8,128)}) custom-call(f32[12,16,256]{2,1,0:T(8,128)} %get-tuple-element.8.mid, f32[12,16,256]{2,1,0:T(8,128)} %get-tuple-element.9.leaf, f32[3,256,256]{2,1,0:T(8,128)} %get-tuple-element.10.gram), custom_call_target="tpu_custom_call" | custom-call | tf_op jit(solution)/shard_map/pallas_call | solution.py:554

commit v3 on v2

--- a/solution.py
+++ b/solution.py
@@ -472,20 +472,23 @@
         copy.wait()
 
 
-def write_out(mid, leaf, gram, mid_out, diag_out, leaf_out, parent_out, leaf_diag_out, sem):
-    copies = [
-        pltpu.make_async_copy(src, dst.at[0], sem.at[n]) for n, (src, dst) in enumerate((
-            (mid, mid_out), (leaf, leaf_out), (gram.at[0], diag_out), (gram.at[1], parent_out),
-            (gram.at[2], leaf_diag_out)))]
-    for copy in copies:
+def write_out(mid, leaf, gram, mid_out, diag_out, leaf_out, parent_out, leaf_diag_out, columns, blocks, in_sem, out_sem):
+    parts = (
+        (mid, columns.at[0], mid_out), (leaf, columns.at[1], leaf_out), (gram.at[0], blocks.at[0], diag_out),
+        (gram.at[1], blocks.at[1], parent_out), (gram.at[2], blocks.at[2], leaf_diag_out))
+    ins = [pltpu.make_async_copy(src, held, in_sem.at[n]) for n, (src, held, _) in enumerate(parts)]
+    outs = [pltpu.make_async_copy(held, dst.at[0], out_sem.at[n]) for n, (_, held, dst) in enumerate(parts)]
+    for copy in ins:
         copy.start()
-    for copy in copies:
+    for came, goes in zip(ins, outs):
+        came.wait()
+        goes.start()
+    for copy in outs:
         copy.wait()
 
 
 def on_device(sigma_top, mid_struct, leaf_struct, mid_inv, mid_off, leaf_inv, leaf_off):
     hbm = pl.BlockSpec(memory_space=pltpu.HBM)
-    anywhere = pl.BlockSpec(memory_space=pl.ANY)
     dma = pltpu.SemaphoreType.DMA
     middle, leaves, grams = pl.pallas_call(
         kernel,
@@ -554,9 +557,11 @@
     return tuple(pl.pallas_call(
         write_out,
         out_shape=(column, block, column, block, block),
-        in_specs=[anywhere] * 3,
-        out_specs=(anywhere,) * 5,
-        scratch_shapes=[dma((5,))],
+        in_specs=[hbm] * 3,
+        out_specs=(hbm,) * 5,
+        scratch_shapes=[
+            pltpu.VMEM((2, NS1, SLICE, BS), F32), pltpu.VMEM((3, BS, BS), F32), dma((5,)), dma((5,))],
+        compiler_params=pltpu.CompilerParams(vmem_limit_bytes=64 * 1024 * 1024),
     )(middle, leaves, grams))
 
 

time: 135 us -> 100 us (0.74)
  Pallas kernels: 134 us -> 99.3 us
    pallas_call x1, Pallas kernels: 36.9 us -> 2.11 us  [on_device(): pl.pallas_call(write_out, out_shape=(column, block, column, block, block)...]
where the time goes in v3:
time: 100 us
  Pallas kernels  99.3 us (99%)
    pallas_call x1, Pallas kernels, on_device(): pl.pallas_call(kernel, out_shape=(jax.ShapeDtypeStruct((NS1, SLICE, BS),...  97.2 us
    pallas_call x1, Pallas kernels, on_device(): pl.pallas_call(write_out, out_shape=(column, block, column, block, block)...  2.11 us

profile of v3, /device:TPU:1, one launch (start us, length us, event | category | flops | bytes accessed | tf_op | source)
XLA Modules:
  0.0 100.0 jit_solution(12013854145980730689)
XLA Ops:
  0.6 97.2 %shard_map.110 = (f32[12,16,256]{2,1,0:T(8,128)}, f32[12,16,256]{2,1,0:T(8,128)}, f32[3,256,256]{2,1,0:T(8,128)}) custom-call(s32[1,12]{1,0:T(1,128)} %struct_hbm.1, s32[1,6]{1,0:T(1,128)} %leaf_hbm.1, f32[512,512]{1,0:T(8,128)} %sigma_hbm.1, f32[1,256,256]{2,1,0:T(8,128)} %minv_hbm.1, f32[1,12,256,256]{3,2,1,0:T(8,128)} %moff_hbm.1, ...), custom_call_target="tpu_custom_call" | custom-call | tf_op jit(solution)/shard_map/pallas_call | solution.py:493
  97.8 2.1 %shard_map.111 = (f32[1,12,16,256]{3,2,1,0:T(8,128)}, f32[1,256,256]{2,1,0:T(8,128)}, f32[1,12,16,256]{3,2,1,0:T(8,128)}, f32[1,256,256]{2,1,0:T(8,128)}, f32[1,256,256]{2,1,0:T(8,128)}) custom-call(f32[12,16,256]{2,1,0:T(8,128)} %get-tuple-element.8.mid, f32[12,16,256]{2,1,0:T(8,128)} %get-tuple-element.9.leaf, f32[3,256,256]{2,1,0:T(8,128)} %get-tuple-element.10.gram), custom_call_target="tpu_custom_call" | custom-call | tf_op jit(solution)/shard_map/pallas_call | solution.py:557

commit v4 on v3

--- a/solution.py
+++ b/solution.py
@@ -17,8 +17,10 @@
 SLICE = 16
 SLOTS = 17
 HALF = SUB // 2
-PIECES = ((0, 0, 8), (0, 8, 9), (1, 0, 8), (1, 8, 9))
+THIN = SLICE // 2
+PIECES = ((0, 8), (8, 9))
 ROWS = NS1 * SUB
+HROWS = NS1 * HALF
 OUTS = NS1 + NS2
 
 
@@ -40,20 +42,22 @@
 def kernel(
     struct_hbm, leaf_hbm, sigma_hbm, minv_hbm, moff_hbm, linv_hbm, loff_hbm,
     mid_hbm, column_hbm, gram_hbm,
-    struct, leaf, sigma, packed, extra, gathered, moff, loff, first_raw, minv, linv, vblocks, v0_hi, v0_lo, base,
-    w_hi, w_lo, wt_hi, wt_lo, a_hi, a_lo, ysum, ysend, yrecv, ycomb, gsend, grecv, gcomb, gred, gexch, gall,
-    column_out, gram_out, out_sem,
-    load_sem, pack_send, pack_recv, extra_send, extra_recv, z_send, right_recv, left_recv,
-    pair_send, pair_recv, y_send_sem, y_recv_sem, g_send_sem, g_recv_sem,
+    struct, leaf, sigma, packed, extra, gathered_a, gathered_b, moff_c, loff_c, moff_r, loff_r, first_raw, minv, linv,
+    vblocks_c, vblocks_r, v0_hi, v0_lo, base, wc_hi, wc_lo, wr_hi, wr_lo, wt_hi, wt_lo, a_hi, a_lo, y1, y2, gram_sum,
+    y1send, y1recv, y1comb, y2send, y2recv, y2comb, gsend, grecv, gcomb, gred, gexch, gall,
+    column_out, gram_out, out_sem, load_sem, pack_send, pack_recv, extra_send, extra_recv, z_send, right_recv, left_recv,
+    pair_send, pair_recv, y1_send_sem, y1_recv_sem, y2_send_sem, y2_recv_sem, g_send_sem, g_recv_sem,
 ):
     branch = lax.axis_index("branch")
     grid = lax.axis_index("grid")
     z, core = branch // 2, branch % 2
     y, x = grid // SIDE, grid % SIDE
 
-    def slots(which_core, source, half, slot, size=None):
-        start = ((which_core * RING + source) * 2 + half) * SLOTS + slot
-        return gathered.at[start] if size is None else gathered.at[pl.ds(start, size)]
+    gathered = (gathered_a, gathered_b)
+
+    def slots(half, which_core, source, slot, size=None):
+        start = (which_core * RING + source) * SLOTS + slot
+        return gathered[half].at[start] if size is None else gathered[half].at[pl.ds(start, size)]
 
     def at_grid(index):
         return {"branch": branch, "grid": index}
@@ -75,19 +79,21 @@
         pltpu.make_async_copy(minv_hbm.at[0], minv, load_sem.at[0]),
         pltpu.make_async_copy(linv_hbm.at[0], linv, load_sem.at[1]),
         pltpu.make_async_copy(loff_hbm.at[0, 0], first_raw, load_sem.at[2]),
-        pltpu.make_async_copy(moff_hbm.at[0, :, pl.ds(row_c, SUB), :], moff.at[0], load_sem.at[3]),
-        pltpu.make_async_copy(loff_hbm.at[0, pl.ds(1, NS2), pl.ds(row_c, SUB), :], loff.at[0], load_sem.at[4]),
+        pltpu.make_async_copy(moff_hbm.at[0, :, pl.ds(row_c, SUB), :], moff_c, load_sem.at[3]),
+        pltpu.make_async_copy(loff_hbm.at[0, pl.ds(1, NS2), pl.ds(row_c, SUB), :], loff_c, load_sem.at[4]),
     ]
     for m in range(SIDE):
-        row_r = pl.multiple_of(m * SUB + x * SLICE, SLICE)
-        into = pl.ds(m * SLICE, SLICE)
-        loads.append(pltpu.make_async_copy(
-            moff_hbm.at[0, :, pl.ds(row_r, SLICE), :], moff.at[1, :, into, :], load_sem.at[5 + m]))
-        loads.append(pltpu.make_async_copy(
-            loff_hbm.at[0, pl.ds(1, NS2), pl.ds(row_r, SLICE), :], loff.at[1, :, into, :], load_sem.at[9 + m]))
-    loads.append(pltpu.make_async_copy(struct_hbm, struct, load_sem.at[13]))
-    loads.append(pltpu.make_async_copy(leaf_hbm, leaf, load_sem.at[14]))
-    own = pltpu.make_async_copy(sigma_hbm, sigma, load_sem.at[15])
+        for half in range(2):
+            row_r = pl.multiple_of(m * SUB + x * SLICE + half * THIN, THIN)
+            into = pl.ds(m * THIN, THIN)
+            loads.append(pltpu.make_async_copy(
+                moff_hbm.at[0, :, pl.ds(row_r, THIN), :], moff_r.at[half, :, into, :], load_sem.at[len(loads)]))
+            loads.append(pltpu.make_async_copy(
+                loff_hbm.at[0, pl.ds(1, NS2), pl.ds(row_r, THIN), :], loff_r.at[half, :, into, :],
+                load_sem.at[len(loads)]))
+    loads.append(pltpu.make_async_copy(struct_hbm, struct, load_sem.at[21]))
+    loads.append(pltpu.make_async_copy(leaf_hbm, leaf, load_sem.at[22]))
+    own = pltpu.make_async_copy(sigma_hbm, sigma, load_sem.at[23])
     own.start()
 
     barrier = pltpu.get_barrier_semaphore()
@@ -115,8 +121,9 @@
         for side, value in ((2 * half, even), (2 * half + 1, odd)):
             for m in range(SIDE):
                 for xx in range(SIDE):
-                    start = m * SUB + xx * SLICE
-                    packed[m // 2, side * SIDE + xx, m % 2 * SLICE:(m % 2 + 1) * SLICE, :] = value[start:start + SLICE, :]
+                    for part in range(2):
+                        start = m * SUB + xx * SLICE + part * THIN
+                        packed[part, side * SIDE + xx, m * THIN:(m + 1) * THIN, :] = value[start:start + THIN, :]
 
     @pl.when(grid == branch)
     def _():
@@ -125,18 +132,19 @@
             for side, turned in ((2 * half, value), (2 * half + 1, pltpu.roll(value, SUB, 1))):
                 for m in range(SIDE):
                     for xx in range(SIDE):
-                        start = m * SUB + xx * SLICE
-                        extra[m // 2, side * SIDE + xx, m % 2 * SLICE:(m % 2 + 1) * SLICE, :] = turned[start:start + SLICE, :]
+                        for part in range(2):
+                            start = m * SUB + xx * SLICE + part * THIN
+                            extra[part, side * SIDE + xx, m * THIN:(m + 1) * THIN, :] = turned[start:start + THIN, :]
 
     pl.semaphore_wait(barrier, SIDE * SIDE + 2)
 
     for half in range(2):
-        pltpu.make_async_copy(packed.at[half, grid], slots(core, z, half, grid), pack_recv.at[half]).start()
+        pltpu.make_async_copy(packed.at[half, grid], slots(half, core, z, grid), pack_recv.at[half]).start()
 
         def hand_out(step, carry):
             to = lax.rem(grid + step, SIDE * SIDE)
             pltpu.make_async_remote_copy(
-                src_ref=packed.at[half, to], dst_ref=slots(core, z, half, grid), send_sem=pack_send,
+                src_ref=packed.at[half, to], dst_ref=slots(half, core, z, grid), send_sem=pack_send,
                 recv_sem=pack_recv.at[half], device_id=at_grid(to), device_id_type=MESH).start()
             return carry
 
@@ -144,7 +152,7 @@
 
         @pl.when(grid == branch)
         def _():
-            own_slot = slots(core, z, half, SLOTS - 1)
+            own_slot = slots(half, core, z, SLOTS - 1)
             pltpu.make_async_copy(extra.at[half, grid], own_slot, extra_recv.at[half]).start()
 
             def hand_extra(step, carry):
@@ -156,32 +164,45 @@
 
             lax.fori_loop(1, SIDE * SIDE, hand_extra, 0)
 
-    def piece_of(source, piece):
-        half, start, size = PIECES[piece]
-        return slots(core, source, half, start, size)
-
-    def pass_on(source, piece, to, recv_sem):
-        ref = piece_of(source, piece)
+    def piece_of(half, source, piece):
+        return slots(half, core, source, *PIECES[piece])
+
+    def pass_on(half, source, piece, to, recv_sem):
+        ref = piece_of(half, source, piece)
         pltpu.make_async_remote_copy(
             src_ref=ref, dst_ref=ref, send_sem=z_send, recv_sem=recv_sem, device_id=to, device_id_type=MESH).start()
 
-    def to_pair(source, piece):
-        ref = piece_of(source, piece)
+    def to_pair(half, source, piece):
+        ref = piece_of(half, source, piece)
         pltpu.make_async_remote_copy(
-            src_ref=ref, dst_ref=ref, send_sem=pair_send, recv_sem=pair_recv, device_id=pair,
+            src_ref=ref, dst_ref=ref, send_sem=pair_send, recv_sem=pair_recv.at[half], device_id=pair,
             device_id_type=MESH).start()
 
     def await_bytes(ref, sem):
         pltpu.make_async_copy(ref, ref, sem).wait()
 
-    for piece in range(4):
-        half = PIECES[piece][0]
-        if piece % 2 == 0:
-            await_bytes(slots(core, z, half, 0, SIDE * SIDE), pack_recv.at[half])
-            await_bytes(slots(core, z, half, SLOTS - 1), extra_recv.at[half])
-        pass_on(z, piece, up, right_recv.at[1, piece])
-        pass_on(z, piece, down, left_recv.at[1, piece])
-        to_pair(z, piece)
+    def begin(half):
+        await_bytes(slots(half, core, z, 0, SIDE * SIDE), pack_recv.at[half])
+        await_bytes(slots(half, core, z, SLOTS - 1), extra_recv.at[half])
+        for piece in range(2):
+            pass_on(half, z, piece, up, right_recv.at[half, 1, piece])
+            pass_on(half, z, piece, down, left_recv.at[half, 1, piece])
+            to_pair(half, z, piece)
+
+    def gather_step(half, step):
+        below = lax.rem(z + RING - step, RING)
+        above = lax.rem(z + step, RING)
+        for piece in range(2):
+            if step < 4 or piece == 0:
+                await_bytes(piece_of(half, below, piece), right_recv.at[half, step, piece])
+                if step < 3 or (step == 3 and piece == 0):
+                    pass_on(half, below, piece, up, right_recv.at[half, step + 1, piece])
+                to_pair(half, below, piece)
+            if step < 4 or piece == 1:
+                await_bytes(piece_of(half, above, piece), left_recv.at[half, step, piece])
+                if step < 3 or (step == 3 and piece == 1):
+                    pass_on(half, above, piece, down, left_recv.at[half, step + 1, piece])
+                to_pair(half, above, piece)
 
     def leaf_of(k):
         found, index = 0, 0
@@ -191,91 +212,91 @@
             index = index + same * t
         return jnp.minimum(index, NS2 - 1), found.astype(F32)
 
-    def factors():
+    def factors_c():
         for load in loads:
             load.wait()
         minv_s = split(minv[...])
         linv_s = split(linv[...])
         v0_s = split(product(split(first_raw[...]), linv_s))
         v0_hi[...], v0_lo[...] = v0_s
-        for part in range(2):
-            vblocks[part] = product(split(loff[part].reshape(NS2 * SUB, BS)), linv_s).reshape(NS2, SUB, BS)
+        vblocks_c[...] = product(split(loff_c[...].reshape(NS2 * SUB, BS)), linv_s).reshape(NS2, SUB, BS)
+
+        def rows(q, carry):
+            u = product(split(moff_c[pl.ds(q * 4, 4)].reshape(BS, BS)), split(minv[...]))
+            u_s = split(u)
+            uv = product(u_s, (v0_hi[...], v0_lo[...]))
+            spread = []
+            for j in range(4):
+                index, mark = leaf_of(q * 4 + j)
+                spread.append(vblocks_c[index] * mark)
+            t_s = split(jnp.concatenate(spread, axis=0) - uv)
+            at = pl.ds(pl.multiple_of(q * BS, BS), BS)
+            for kind, pieces in ((0, u_s), (1, t_s)):
+                wc_hi[at, kind * BS:(kind + 1) * BS] = pieces[0]
+                wc_lo[at, kind * BS:(kind + 1) * BS] = pieces[1]
+            return carry
+
+        lax.fori_loop(0, 3, rows, 0)
+
+    def factors_r():
+        minv_s = split(minv[...])
+        linv_s = split(linv[...])
+        v0_s = (v0_hi[...], v0_lo[...])
         square = product_t(minv_s, minv_s)
         base[0] = square
         turned = product(split(square), v0_s)
         base[1] = -turned
         base[2] = product_t(linv_s, linv_s) + product_t(v0_s, split(turned))
-        for part in range(2):
-            def rows(q, carry):
-                raw = moff[part, pl.ds(q * 4, 4)].reshape(BS, BS)
-                u = product(split(raw), (split(minv[...])))
-                u_s = split(u)
-                uv = product(u_s, (v0_hi[...], v0_lo[...]))
-                spread = []
-                for j in range(4):
-                    index, mark = leaf_of(q * 4 + j)
-                    spread.append(vblocks[part, index] * mark)
-                t = jnp.concatenate(spread, axis=0) - uv
-                t_s = split(t)
-                at = pl.ds(pl.multiple_of(q * BS, BS), BS)
-                for kind, pieces in ((0, u_s), (1, t_s)):
-                    w_hi[part, at, kind * BS:(kind + 1) * BS] = pieces[0]
-                    w_lo[part, at, kind * BS:(kind + 1) * BS] = pieces[1]
-                if part == 1:
-                    for kind, value in ((0, u), (1, t)):
-                        high, low = split(value.T)
-                        wt_hi[kind * BS:(kind + 1) * BS, at] = high
-                        wt_lo[kind * BS:(kind + 1) * BS, at] = low
-                return carry
-            lax.fori_loop(0, 3, rows, 0)
-
-    factors()
-
-    for step in range(1, 5):
-        below = lax.rem(z + RING - step, RING)
-        above = lax.rem(z + step, RING)
-        for piece in range(4):
-            if step < 4 or piece < 2:
-                await_bytes(piece_of(below, piece), right_recv.at[step, piece])
-                if step < 3 or (step == 3 and piece < 2):
-                    pass_on(below, piece, up, right_recv.at[step + 1, piece])
-                to_pair(below, piece)
-            if step < 4 or piece >= 2:
-                await_bytes(piece_of(above, piece), left_recv.at[step, piece])
-                if step < 3 or (step == 3 and piece >= 2):
-                    pass_on(above, piece, down, left_recv.at[step + 1, piece])
-                to_pair(above, piece)
-    await_bytes(slots(1 - core, 0, 0, 0, 2 * RING * SLOTS), pair_recv)
+        vblocks_r[...] = product(split(loff_r[...].reshape(2 * NS2 * HALF, BS)), linv_s).reshape(2 * NS2, HALF, BS)
+
+        def rows(half, carry):
+            u = product(split(moff_r[half].reshape(HROWS, BS)), split(minv[...]))
+            u_s = split(u)
+            uv = product(u_s, (v0_hi[...], v0_lo[...]))
+            spread = []
+            for k in range(NS1):
+                index, mark = leaf_of(k)
+                spread.append(vblocks_r[half * NS2 + index] * mark)
+            t = jnp.concatenate(spread, axis=0) - uv
+            t_s = split(t)
+            at = pl.ds(pl.multiple_of(half * HROWS, HROWS), HROWS)
+            for kind, value, pieces in ((0, u, u_s), (1, t, t_s)):
+                wr_hi[at, kind * BS:(kind + 1) * BS] = pieces[0]
+                wr_lo[at, kind * BS:(kind + 1) * BS] = pieces[1]
+                high, low = split(value.T)
+                wt_hi[half, kind * BS:(kind + 1) * BS, :] = high
+                wt_lo[half, kind * BS:(kind + 1) * BS, :] = low
+            return carry
+
+        lax.fori_loop(0, 2, rows, 0)
 
     narrow = lax.broadcasted_iota(jnp.int32, (HALF, 128), 1) < SUB
 
-    def select(k, carry):
-        si = struct[0, k]
-        gi, ai = si >> 1, si & 1
-        for p in range(NS1 // 2):
-            sides = [[], []]
-            for h in range(2):
-                sj = struct[0, 2 * p + h]
-                bj, cj = sj >> 1, sj & 1
-                beyond = (gi > bj).astype(jnp.int32)
-                plain = (cj == (ai ^ beyond)).astype(jnp.int32)
-                own = ((gi == bj).astype(jnp.int32)) * (1 - ai) * cj
-                slot = own * (SLOTS - 1) + (1 - own) * gi
-                there = (1 - own) * ai
-                weight = (plain + own).astype(F32) * (1.0 - 0.5 * (si == sj).astype(F32))
-                stay = (there == h).astype(F32)
-                for half in range(2):
-                    share = gathered[(((bj & 1) * RING + (bj >> 1)) * 2 + half) * SLOTS + slot]
-                    sides[half].append(
-                        share * (weight * stay) + pltpu.roll(share, SUB, 1) * (weight * (1.0 - stay)))
-            for half in range(2):
-                row = pl.ds(pl.multiple_of(k * SUB + half * HALF, HALF), HALF)
-                high, low = split(jnp.where(narrow, sides[half][0], sides[half][1]))
+    def select(half):
+        def row_block(k, carry):
+            si = struct[0, k]
+            gi, ai = si >> 1, si & 1
+            for p in range(NS1 // 2):
+                sides = []
+                for h in range(2):
+                    sj = struct[0, 2 * p + h]
+                    bj, cj = sj >> 1, sj & 1
+                    beyond = (gi > bj).astype(jnp.int32)
+                    plain = (cj == (ai ^ beyond)).astype(jnp.int32)
+                    own = ((gi == bj).astype(jnp.int32)) * (1 - ai) * cj
+                    slot = own * (SLOTS - 1) + (1 - own) * gi
+                    there = (1 - own) * ai
+                    weight = (plain + own).astype(F32) * (1.0 - 0.5 * (si == sj).astype(F32))
+                    stay = (there == h).astype(F32)
+                    share = gathered[half][((bj & 1) * RING + (bj >> 1)) * SLOTS + slot]
+                    sides.append(share * (weight * stay) + pltpu.roll(share, SUB, 1) * (weight * (1.0 - stay)))
+                row = pl.ds(pl.multiple_of(half * HROWS + k * HALF, HALF), HALF)
+                high, low = split(jnp.where(narrow, sides[0], sides[1]))
                 a_hi[row, p * 128:(p + 1) * 128] = high
                 a_lo[row, p * 128:(p + 1) * 128] = low
-        return carry
-
-    lax.fori_loop(0, NS1, select, 0)
+            return carry
+
+        lax.fori_loop(0, NS1, row_block, 0)
 
     def send(src, dst, send_sem, recv_sem, to):
         copy = pltpu.make_async_remote_copy(
@@ -312,14 +333,17 @@
         for slot in (1, 3, 4, 5):
             await_bytes(recv.at[slot], recvs.at[slot])
 
-    def left_rows(r, carry):
-        at = pl.ds(pl.multiple_of(r * BS, BS), BS)
-        ysum[0, pl.ds(r * 4, 4)] = product((a_hi[at, :], a_lo[at, :]), (w_hi[0], w_lo[0])).reshape(4, SUB, 2 * BS)
-        return carry
+    def left_rows(half):
+        at = slice(half * HROWS, (half + 1) * HROWS)
+        for kind in range(2):
+            cols = slice(kind * BS, (kind + 1) * BS)
+            value = product((a_hi[at, :], a_lo[at, :]), (wc_hi[:, cols], wc_lo[:, cols]))
+            y1[half, :, :, cols] = value.reshape(NS1, HALF, BS)
+            term = product((wt_hi[half], wt_lo[half]), split(value))
+            gram_sum[:, cols] = term if half == 0 else gram_sum[:, cols] + term
 
     def gram(left, right):
-        at = slice(left * BS, (left + 1) * BS)
-        return product((wt_hi[at, :], wt_lo[at, :]), split(ysum[0, :, :, right * BS:(right + 1) * BS].reshape(ROWS, BS)))
+        return gram_sum[left * BS:(left + 1) * BS, right * BS:(right + 1) * BS]
 
     def put_gram(index, value):
         for part in range(16):
@@ -332,29 +356,42 @@
     def g_chunk(axis):
         return lambda t, h: gsend.at[axis, t, h]
 
-    def y_chunk(axis):
-        return lambda t, h: ysend.at[axis, t, h]
-
     def g_ring(axis):
         return axis, g_chunk(axis), grecv.at[axis], g_send_sem.at[axis], g_recv_sem.at[axis]
 
-    def y_ring(axis):
-        return axis, y_chunk(axis), yrecv.at[axis], y_send_sem.at[axis], y_recv_sem.at[axis]
-
-    def pack_rows(source, axis):
+    def y1_ring(half):
+        return 1, lambda t, h: y1send.at[half, t, h], y1recv.at[half], y1_send_sem.at[half], y1_recv_sem.at[half]
+
+    y2_ring = (0, lambda t, h: y2send.at[t, h], y2recv, y2_send_sem, y2_recv_sem)
+
+    def pack_rows(blocks, put, thickness):
         for n in range(OUTS):
-            if n < NS1:
-                value = ysum[source, n, :, 0:BS]
-            else:
-                value = ysum[source, leaf[0, n - NS1], :, BS:2 * BS]
+            value = blocks(n) if n < NS1 else blocks(None, leaf[0, n - NS1])
             for t in range(SIDE):
-                ysend[axis, t, n // 9, n % 9] = value[t * SLICE:(t + 1) * SLICE, :]
+                put(t, n // 9, n % 9, value[t * thickness:(t + 1) * thickness, :])
+
+    def pack_y1(half):
+        def blocks(n, found=None):
+            return y1[half, n, :, 0:BS] if found is None else y1[half, found, :, BS:2 * BS]
+
+        def put(t, side, n, value):
+            y1send[half, t, side, n] = value
+
+        pack_rows(blocks, put, THIN)
+
+    def pack_y2():
+        def blocks(n, found=None):
+            return y2[n, :, 0:BS] if found is None else y2[found, :, BS:2 * BS]
+
+        def put(t, side, n, value):
+            y2send[t, side, n] = value
+
+        pack_rows(blocks, put, SLICE)
 
     def right_rows(r, carry):
         at = pl.ds(pl.multiple_of(r * BS, BS), BS)
-        ysum[1, pl.ds(r * 4, 4)] = product_t((a_hi[:, at], a_lo[:, at]), (w_hi[1], w_lo[1])).reshape(4, SUB, 2 * BS)
+        y2[pl.ds(r * 4, 4)] = product_t((a_hi[:, at], a_lo[:, at]), (wr_hi[...], wr_lo[...])).reshape(4, SUB, 2 * BS)
         return carry
-
 
     def g_sum_and_exchange(axis):
         recv, recvs, sends = grecv.at[axis], g_recv_sem.at[axis], g_send_sem.at[axis]
@@ -397,12 +434,36 @@
     def g_second(axis):
         second_hop(axis, g_chunk(axis), grecv.at[axis], gcomb.at[axis], g_send_sem.at[axis], g_recv_sem.at[axis])
 
-    def y_second(axis):
-        second_hop(axis, y_chunk(axis), yrecv.at[axis], ycomb.at[axis], y_send_sem.at[axis], y_recv_sem.at[axis])
-
-    lax.fori_loop(0, 3, left_rows, 0)
-    pack_rows(0, 1)
-    first_hop(*y_ring(1))
+    def y1_second(half):
+        axis, chunk, recv, sends, recvs = y1_ring(half)
+        second_hop(axis, chunk, recv, y1comb.at[half], sends, recvs)
+
+    def y2_second():
+        axis, chunk, recv, sends, recvs = y2_ring
+        second_hop(axis, chunk, recv, y2comb, sends, recvs)
+
+    begin(0)
+    factors_c()
+    gather_step(0, 1)
+    factors_r()
+    gather_step(0, 2)
+    gather_step(0, 3)
+    begin(1)
+    gather_step(0, 4)
+    await_bytes(slots(0, 1 - core, 0, 0, RING * SLOTS), pair_recv.at[0])
+    select(0)
+    left_rows(0)
+    gather_step(1, 1)
+    pack_y1(0)
+    first_hop(*y1_ring(0))
+    direct_hop(*y1_ring(0))
+    gather_step(1, 2)
+    y1_second(0)
+    gather_step(1, 3)
+    gather_step(1, 4)
+    await_bytes(slots(1, 1 - core, 0, 0, RING * SLOTS), pair_recv.at[1])
+    select(1)
+    left_rows(1)
     h00 = gram(0, 0)
     put_gram(0, h00 + h00.T)
     put_gram(1, gram(0, 1) + gram(1, 0).T)
@@ -411,35 +472,39 @@
     for axis in (0, 1):
         first_hop(*g_ring(axis))
         direct_hop(*g_ring(axis))
-    direct_hop(*y_ring(1))
+    pack_y1(1)
+    first_hop(*y1_ring(1))
     lax.fori_loop(0, 3, right_rows, 0)
-    pack_rows(1, 0)
+    pack_y2()
+    first_hop(*y2_ring)
     for axis in (0, 1):
         g_second(axis)
-    first_hop(*y_ring(0))
-    y_second(1)
+    direct_hop(*y1_ring(1))
+    direct_hop(*y2_ring)
     for axis in (0, 1):
         g_sum_and_exchange(axis)
-    direct_hop(*y_ring(0))
+    y1_second(1)
     for axis in (0, 1):
         g_exchange_on(axis)
-    y_second(0)
+    y2_second()
     for axis in (0, 1):
         g_spread(axis)
     for axis in (0, 1):
         g_spread_on(axis)
 
-    for axis in (1, 0):
-        arrive(yrecv.at[axis], y_recv_sem.at[axis])
-    for half, direct, through in ((0, 3, 4), (1, 1, 5)):
-        total = 0.0
-        for axis in (0, 1):
-            total = total + ((ysend[axis, place[axis], half] + yrecv[axis, direct]) + yrecv[axis, through])
-        ycomb[2, half] = -total
+    for half in range(2):
+        arrive(y1recv.at[half], y1_recv_sem.at[half])
+    arrive(y2recv, y2_recv_sem)
+    for side, direct, through in ((0, 3, 4), (1, 1, 5)):
+        total = (y2send[x, side] + y2recv[direct]) + y2recv[through]
+        for half in range(2):
+            rows = slice(half * THIN, (half + 1) * THIN)
+            part = (y1send[half, y, side] + y1recv[half, direct]) + y1recv[half, through]
+            y2comb[2 + side, :, rows, :] = -(total[:, rows, :] + part)
     for n in range(NS1):
-        column_out[0, n] = ycomb[2, n // 9, n % 9]
+        column_out[0, n] = y2comb[2 + n // 9, n % 9]
         index, mark = leaf_of(n)
-        column_out[1, n] = ycomb[2, 1, index + (NS1 - 9)] * mark
+        column_out[1, n] = y2comb[3, index + (NS1 - 9)] * mark
 
     outs = [
         pltpu.make_async_copy(column_out.at[0], mid_hbm, out_sem.at[0]),
@@ -466,8 +531,8 @@
         for half in range(2):
             await_bytes(extra.at[half, pl.ds(0, SIDE * SIDE - 1)], extra_send)
 
-    await_bytes(slots(core, 0, 0, 0, 2 * (RING - 1) * SLOTS), z_send)
-    await_bytes(slots(core, 0, 0, 0, 2 * RING * SLOTS), pair_send)
+    await_bytes(slots(0, 0, 0, 0, 2 * (RING - 1) * SLOTS), z_send)
+    await_bytes(slots(0, 0, 0, 0, 2 * RING * SLOTS), pair_send)
     for copy in outs:
         copy.wait()
 
@@ -505,26 +570,37 @@
             pltpu.VMEM((2 * BS, 2 * BS), F32),
             pltpu.VMEM((2, SIDE * SIDE, HALF, 128), F32),
             pltpu.VMEM((2, SIDE * SIDE, HALF, 128), F32),
-            pltpu.VMEM((4 * RING * SLOTS, HALF, 128), F32),
-            pltpu.VMEM((2, NS1, SUB, BS), F32),
-            pltpu.VMEM((2, NS2, SUB, BS), F32),
+            pltpu.VMEM((2 * RING * SLOTS, HALF, 128), F32),
+            pltpu.VMEM((2 * RING * SLOTS, HALF, 128), F32),
+            pltpu.VMEM((NS1, SUB, BS), F32),
+            pltpu.VMEM((NS2, SUB, BS), F32),
+            pltpu.VMEM((2, NS1, HALF, BS), F32),
+            pltpu.VMEM((2, NS2, HALF, BS), F32),
             pltpu.VMEM((BS, BS), F32),
             pltpu.VMEM((BS, BS), F32),
             pltpu.VMEM((BS, BS), F32),
-            pltpu.VMEM((2, NS2, SUB, BS), F32),
+            pltpu.VMEM((NS2, SUB, BS), F32),
+            pltpu.VMEM((2 * NS2, HALF, BS), F32),
             pltpu.VMEM((BS, BS), BF16),
             pltpu.VMEM((BS, BS), BF16),
             pltpu.VMEM((3, BS, BS), F32),
-            pltpu.VMEM((2, ROWS, 2 * BS), BF16),
-            pltpu.VMEM((2, ROWS, 2 * BS), BF16),
-            pltpu.VMEM((2 * BS, ROWS), BF16),
-            pltpu.VMEM((2 * BS, ROWS), BF16),
+            pltpu.VMEM((ROWS, 2 * BS), BF16),
+            pltpu.VMEM((ROWS, 2 * BS), BF16),
+            pltpu.VMEM((ROWS, 2 * BS), BF16),
+            pltpu.VMEM((ROWS, 2 * BS), BF16),
+            pltpu.VMEM((2, 2 * BS, HROWS), BF16),
+            pltpu.VMEM((2, 2 * BS, HROWS), BF16),
             pltpu.VMEM((ROWS, ROWS), BF16),
             pltpu.VMEM((ROWS, ROWS), BF16),
-            pltpu.VMEM((2, NS1, SUB, 2 * BS), F32),
-            pltpu.VMEM((2, SIDE, 2, 9, SLICE, BS), F32),
-            pltpu.VMEM((2, 6, 9, SLICE, BS), F32),
-            pltpu.VMEM((3, 2, 9, SLICE, BS), F32),
+            pltpu.VMEM((2, NS1, HALF, 2 * BS), F32),
+            pltpu.VMEM((NS1, SUB, 2 * BS), F32),
+            pltpu.VMEM((2 * BS, 2 * BS), F32),
+            pltpu.VMEM((2, SIDE, 2, 9, THIN, BS), F32),
+            pltpu.VMEM((2, 6, 9, THIN, BS), F32),
+            pltpu.VMEM((2, 2, 9, THIN, BS), F32),
+            pltpu.VMEM((SIDE, 2, 9, SLICE, BS), F32),
+            pltpu.VMEM((6, 9, SLICE, BS), F32),
+            pltpu.VMEM((4, 9, SLICE, BS), F32),
             pltpu.VMEM((2, SIDE, 2, 48, BS), F32),
             pltpu.VMEM((2, 6, 48, BS), F32),
             pltpu.VMEM((2, 2, 48, BS), F32),
@@ -534,18 +610,20 @@
             pltpu.VMEM((2, NS1, SLICE, BS), F32),
             pltpu.VMEM((3, BS, BS), F32),
             dma((3,)),
-            dma((16,)),
+            dma((24,)),
             dma,
             dma((2,)),
             dma,
             dma((2,)),
             dma,
-            dma((5, 4)),
-            dma((5, 4)),
+            dma((2, 5, 2)),
+            dma((2, 5, 2)),
             dma,
-            dma,
+            dma((2,)),
             dma((2, 6)),
             dma((2, 6)),
+            dma((6,)),
+            dma((6,)),
             dma((2, 14)),
             dma((2, 14)),
         ],

time: 100 us -> 108 us (1.080)
  Pallas kernels: 99.3 us -> 107 us
    pallas_call x1, Pallas kernels: 97.2 us -> 105 us  [on_device(): pl.pallas_call(kernel, out_shape=(jax.ShapeDtypeStruct((NS1, SLICE, BS),...]
where the time goes in v4:
time: 108 us
  Pallas kernels  107 us (99%)
    pallas_call x1, Pallas kernels, on_device(): pl.pallas_call(kernel, out_shape=(jax.ShapeDtypeStruct((NS1, SLICE, BS),...  105 us

profile of v4, /device:TPU:1, one launch (start us, length us, event | category | flops | bytes accessed | tf_op | source)
XLA Modules:
  0.0 107.6 jit_solution(5262603243329279431)
XLA Ops:
  0.6 104.9 %shard_map.110 = (f32[12,16,256]{2,1,0:T(8,128)}, f32[12,16,256]{2,1,0:T(8,128)}, f32[3,256,256]{2,1,0:T(8,128)}) custom-call(s32[1,12]{1,0:T(1,128)} %struct_hbm.1, s32[1,6]{1,0:T(1,128)} %leaf_hbm.1, f32[512,512]{1,0:T(8,128)} %sigma_hbm.1, f32[1,256,256]{2,1,0:T(8,128)} %minv_hbm.1, f32[1,12,256,256]{3,2,1,0:T(8,128)} %moff_hbm.1, ...), custom_call_target="tpu_custom_call" | custom-call | tf_op jit(solution)/shard_map/pallas_call | solution.py:558
  105.5 2.1 %shard_map.111 = (f32[1,12,16,256]{3,2,1,0:T(8,128)}, f32[1,256,256]{2,1,0:T(8,128)}, f32[1,12,16,256]{3,2,1,0:T(8,128)}, f32[1,256,256]{2,1,0:T(8,128)}, f32[1,256,256]{2,1,0:T(8,128)}) custom-call(f32[12,16,256]{2,1,0:T(8,128)} %get-tuple-element.8.mid, f32[12,16,256]{2,1,0:T(8,128)} %get-tuple-element.9.leaf, f32[3,256,256]{2,1,0:T(8,128)} %get-tuple-element.10.gram), custom_call_target="tpu_custom_call" | custom-call | tf_op jit(solution)/shard_map/pallas_call | solution.py:635

commit v5 on v3

--- a/solution.py
+++ b/solution.py
@@ -17,7 +17,8 @@
 SLICE = 16
 SLOTS = 17
 HALF = SUB // 2
-PIECES = ((0, 0, 8), (0, 8, 9), (1, 0, 8), (1, 8, 9))
+TILES = 2 * SLOTS - 1
+PIECES = ((0, 0, 8), (0, 8, 9), (1, 0, 8), (1, 8, 8))
 ROWS = NS1 * SUB
 OUTS = NS1 + NS2
 
@@ -52,7 +53,7 @@
     y, x = grid // SIDE, grid % SIDE
 
     def slots(which_core, source, half, slot, size=None):
-        start = ((which_core * RING + source) * 2 + half) * SLOTS + slot
+        start = (which_core * RING + source) * TILES + half * SLOTS + slot
         return gathered.at[start] if size is None else gathered.at[pl.ds(start, size)]
 
     def at_grid(index):
@@ -122,15 +123,18 @@
     def _():
         for half in range(2):
             value = sigma[0:BS, BS + half * 128:BS + (half + 1) * 128]
-            for side, turned in ((2 * half, value), (2 * half + 1, pltpu.roll(value, SUB, 1))):
-                for m in range(SIDE):
+            turned = pltpu.roll(value, SUB, 1)
+            for side, upper, lower in ((2 * half, value, turned), (2 * half + 1, turned, value)):
+                for m in range(2):
                     for xx in range(SIDE):
                         start = m * SUB + xx * SLICE
-                        extra[m // 2, side * SIDE + xx, m % 2 * SLICE:(m % 2 + 1) * SLICE, :] = turned[start:start + SLICE, :]
+                        extra[side * SIDE + xx, m * SLICE:(m + 1) * SLICE, :] = jnp.where(
+                            lane[0:SLICE] < SUB, upper[start:start + SLICE, :],
+                            lower[2 * SUB + start:2 * SUB + start + SLICE, :])
 
     pl.semaphore_wait(barrier, SIDE * SIDE + 2)
 
-    for half in range(2):
+    def exchange(half):
         pltpu.make_async_copy(packed.at[half, grid], slots(core, z, half, grid), pack_recv.at[half]).start()
 
         def hand_out(step, carry):
@@ -142,19 +146,20 @@
 
         lax.fori_loop(1, SIDE * SIDE, hand_out, 0)
 
-        @pl.when(grid == branch)
-        def _():
-            own_slot = slots(core, z, half, SLOTS - 1)
-            pltpu.make_async_copy(extra.at[half, grid], own_slot, extra_recv.at[half]).start()
-
-            def hand_extra(step, carry):
-                to = lax.rem(grid + step, SIDE * SIDE)
-                pltpu.make_async_remote_copy(
-                    src_ref=extra.at[half, to], dst_ref=own_slot, send_sem=extra_send,
-                    recv_sem=extra_recv.at[half], device_id=at_grid(to), device_id_type=MESH).start()
-                return carry
-
-            lax.fori_loop(1, SIDE * SIDE, hand_extra, 0)
+        if half == 0:
+            @pl.when(grid == branch)
+            def _():
+                own_slot = slots(core, z, 0, SLOTS - 1)
+                pltpu.make_async_copy(extra.at[grid], own_slot, extra_recv).start()
+
+                def hand_extra(step, carry):
+                    to = lax.rem(grid + step, SIDE * SIDE)
+                    pltpu.make_async_remote_copy(
+                        src_ref=extra.at[to], dst_ref=own_slot, send_sem=extra_send,
+                        recv_sem=extra_recv, device_id=at_grid(to), device_id_type=MESH).start()
+                    return carry
+
+                lax.fori_loop(1, SIDE * SIDE, hand_extra, 0)
 
     def piece_of(source, piece):
         half, start, size = PIECES[piece]
@@ -174,14 +179,18 @@
     def await_bytes(ref, sem):
         pltpu.make_async_copy(ref, ref, sem).wait()
 
+    exchange(0)
     for piece in range(4):
         half = PIECES[piece][0]
         if piece % 2 == 0:
             await_bytes(slots(core, z, half, 0, SIDE * SIDE), pack_recv.at[half])
-            await_bytes(slots(core, z, half, SLOTS - 1), extra_recv.at[half])
+        if piece == 0:
+            await_bytes(slots(core, z, 0, SLOTS - 1), extra_recv)
         pass_on(z, piece, up, right_recv.at[1, piece])
         pass_on(z, piece, down, left_recv.at[1, piece])
         to_pair(z, piece)
+        if piece == 1:
+            exchange(1)
 
     def leaf_of(k):
         found, index = 0, 0
@@ -245,7 +254,7 @@
                 if step < 3 or (step == 3 and piece >= 2):
                     pass_on(above, piece, down, left_recv.at[step + 1, piece])
                 to_pair(above, piece)
-    await_bytes(slots(1 - core, 0, 0, 0, 2 * RING * SLOTS), pair_recv)
+    await_bytes(slots(1 - core, 0, 0, 0, RING * TILES), pair_recv)
 
     narrow = lax.broadcasted_iota(jnp.int32, (HALF, 128), 1) < SUB
 
@@ -260,12 +269,12 @@
                 beyond = (gi > bj).astype(jnp.int32)
                 plain = (cj == (ai ^ beyond)).astype(jnp.int32)
                 own = ((gi == bj).astype(jnp.int32)) * (1 - ai) * cj
-                slot = own * (SLOTS - 1) + (1 - own) * gi
-                there = (1 - own) * ai
                 weight = (plain + own).astype(F32) * (1.0 - 0.5 * (si == sj).astype(F32))
-                stay = (there == h).astype(F32)
                 for half in range(2):
-                    share = gathered[(((bj & 1) * RING + (bj >> 1)) * 2 + half) * SLOTS + slot]
+                    slot = own * (SLOTS - 1) + (1 - own) * (half * SLOTS + gi)
+                    there = own * half + (1 - own) * ai
+                    stay = (there == h).astype(F32)
+                    share = gathered[((bj & 1) * RING + (bj >> 1)) * TILES + slot]
                     sides[half].append(
                         share * (weight * stay) + pltpu.roll(share, SUB, 1) * (weight * (1.0 - stay)))
             for half in range(2):
@@ -321,13 +330,12 @@
         at = slice(left * BS, (left + 1) * BS)
         return product((wt_hi[at, :], wt_lo[at, :]), split(ysum[0, :, :, right * BS:(right + 1) * BS].reshape(ROWS, BS)))
 
-    def put_gram(index, value):
+    def put_gram(first, value):
         for part in range(16):
-            if part * 48 // BS > index or (part * 48 + 47) // BS < index:
-                continue
-            low, high = max(part * 48, index * BS), min(part * 48 + 48, index * BS + BS)
-            gsend[part // 8, part % 8 // 2, part % 2, low - part * 48:high - part * 48, :] = (
-                value[low - index * BS:high - index * BS, :])
+            low, high = max(part * 40, first), min(part * 40 + 40, first + value.shape[0])
+            if low < high:
+                gsend[part // 8, part % 8 // 2, part % 2, low - part * 40:high - part * 40, :] = (
+                    value[low - first:high - first, :])
 
     def g_chunk(axis):
         return lambda t, h: gsend.at[axis, t, h]
@@ -404,10 +412,13 @@
     pack_rows(0, 1)
     first_hop(*y_ring(1))
     h00 = gram(0, 0)
-    put_gram(0, h00 + h00.T)
-    put_gram(1, gram(0, 1) + gram(1, 0).T)
+    h00 = h00 + h00.T
+    put_gram(0, h00[0:128])
+    put_gram(384, gram(0, 1) + gram(1, 0).T)
     h11 = gram(1, 1)
-    put_gram(2, h11 + h11.T)
+    h11 = h11 + h11.T
+    put_gram(128, h11[0:128])
+    put_gram(256, jnp.concatenate([h00[128:, 128:], h11[128:, 128:]], axis=1))
     for axis in (0, 1):
         first_hop(*g_ring(axis))
         direct_hop(*g_ring(axis))
@@ -452,7 +463,13 @@
         far = lax.rem(place[axis] + 2, SIDE)
         await_bytes(gall.at[axis, far, 0], g_recv_sem.at[axis, 12])
         await_bytes(gall.at[axis, far, 1], g_recv_sem.at[axis, 13])
-    gram_out[...] = gall[...].reshape(3, BS, BS) + base[...]
+    total = gall[...].reshape(640, BS)
+    gram_out[1] = total[384:640] + base[1]
+    for index, first in ((0, 0), (2, 128)):
+        upper = total[first:first + 128]
+        gram_out[index, 0:128, :] = upper + base[index, 0:128, :]
+        gram_out[index, 128:256, 0:128] = upper[:, 128:].T + base[index, 128:256, 0:128]
+        gram_out[index, 128:256, 128:256] = total[256:384, first:first + 128] + base[index, 128:256, 128:256]
 
     outs[2].start()
 
@@ -463,11 +480,10 @@
 
     @pl.when(grid == branch)
     def _():
-        for half in range(2):
-            await_bytes(extra.at[half, pl.ds(0, SIDE * SIDE - 1)], extra_send)
-
-    await_bytes(slots(core, 0, 0, 0, 2 * (RING - 1) * SLOTS), z_send)
-    await_bytes(slots(core, 0, 0, 0, 2 * RING * SLOTS), pair_send)
+        await_bytes(extra.at[pl.ds(0, SIDE * SIDE - 1)], extra_send)
+
+    await_bytes(slots(core, 0, 0, 0, (RING - 1) * TILES), z_send)
+    await_bytes(slots(core, 0, 0, 0, RING * TILES), pair_send)
     for copy in outs:
         copy.wait()
 
@@ -504,8 +520,8 @@
             pltpu.SMEM((1, NS2), jnp.int32),
             pltpu.VMEM((2 * BS, 2 * BS), F32),
             pltpu.VMEM((2, SIDE * SIDE, HALF, 128), F32),
-            pltpu.VMEM((2, SIDE * SIDE, HALF, 128), F32),
-            pltpu.VMEM((4 * RING * SLOTS, HALF, 128), F32),
+            pltpu.VMEM((SIDE * SIDE, HALF, 128), F32),
+            pltpu.VMEM((2 * RING * TILES, HALF, 128), F32),
             pltpu.VMEM((2, NS1, SUB, BS), F32),
             pltpu.VMEM((2, NS2, SUB, BS), F32),
             pltpu.VMEM((BS, BS), F32),
@@ -525,12 +541,12 @@
             pltpu.VMEM((2, SIDE, 2, 9, SLICE, BS), F32),
             pltpu.VMEM((2, 6, 9, SLICE, BS), F32),
             pltpu.VMEM((3, 2, 9, SLICE, BS), F32),
-            pltpu.VMEM((2, SIDE, 2, 48, BS), F32),
-            pltpu.VMEM((2, 6, 48, BS), F32),
-            pltpu.VMEM((2, 2, 48, BS), F32),
-            pltpu.VMEM((2, 2, 48, BS), F32),
-            pltpu.VMEM((2, 3, 2, 48, BS), F32),
-            pltpu.VMEM((2, SIDE, 2, 48, BS), F32),
+            pltpu.VMEM((2, SIDE, 2, 40, BS), F32),
+            pltpu.VMEM((2, 6, 40, BS), F32),
+            pltpu.VMEM((2, 2, 40, BS), F32),
+            pltpu.VMEM((2, 2, 40, BS), F32),
+            pltpu.VMEM((2, 3, 2, 40, BS), F32),
+            pltpu.VMEM((2, SIDE, 2, 40, BS), F32),
             pltpu.VMEM((2, NS1, SLICE, BS), F32),
             pltpu.VMEM((3, BS, BS), F32),
             dma((3,)),
@@ -538,7 +554,7 @@
             dma,
             dma((2,)),
             dma,
-            dma((2,)),
+            dma,
             dma,
             dma((5, 4)),
             dma((5, 4)),

time: 100 us -> 98.4 us (0.984)
  Pallas kernels: 99.3 us -> 97.7 us
    pallas_call x1, Pallas kernels: 97.2 us -> 95.6 us  [on_device(): pl.pallas_call(kernel, out_shape=(jax.ShapeDtypeStruct((NS1, SLICE, BS),...]
where the time goes in v5:
time: 98.4 us; the launch traced here: 98.3 us
  Pallas kernels  97.7 us (99%)
    pallas_call x1, Pallas kernels, on_device(): pl.pallas_call(kernel, out_shape=(jax.ShapeDtypeStruct((NS1, SLICE, BS),...  95.6 us
    pallas_call x1, Pallas kernels, on_device(): pl.pallas_call(write_out, out_shape=(column, block, column, block, block)...  2.11 us

profile of v5, /device:TPU:1, one launch (start us, length us, event | category | flops | bytes accessed | tf_op | source)
XLA Modules:
  0.0 98.3 jit_solution(4016708261341375940)
XLA Ops:
  0.6 95.6 %shard_map.110 = (f32[12,16,256]{2,1,0:T(8,128)}, f32[12,16,256]{2,1,0:T(8,128)}, f32[3,256,256]{2,1,0:T(8,128)}) custom-call(s32[1,12]{1,0:T(1,128)} %struct_hbm.1, s32[1,6]{1,0:T(1,128)} %leaf_hbm.1, f32[512,512]{1,0:T(8,128)} %sigma_hbm.1, f32[1,256,256]{2,1,0:T(8,128)} %minv_hbm.1, f32[1,12,256,256]{3,2,1,0:T(8,128)} %moff_hbm.1, ...), custom_call_target="tpu_custom_call" | custom-call | tf_op jit(solution)/shard_map/pallas_call | solution.py:509
  96.2 2.1 %shard_map.111 = (f32[1,12,16,256]{3,2,1,0:T(8,128)}, f32[1,256,256]{2,1,0:T(8,128)}, f32[1,12,16,256]{3,2,1,0:T(8,128)}, f32[1,256,256]{2,1,0:T(8,128)}, f32[1,256,256]{2,1,0:T(8,128)}) custom-call(f32[12,16,256]{2,1,0:T(8,128)} %get-tuple-element.8.mid, f32[12,16,256]{2,1,0:T(8,128)} %get-tuple-element.9.leaf, f32[3,256,256]{2,1,0:T(8,128)} %get-tuple-element.10.gram), custom_call_target="tpu_custom_call" | custom-call | tf_op jit(solution)/shard_map/pallas_call | solution.py:573

commit v6 on v5

--- a/solution.py
+++ b/solution.py
@@ -459,6 +459,17 @@
     ]
     outs[0].start()
     outs[1].start()
+    for copy in started[:-4]:
+        copy.wait_send()
+    for half in range(2):
+        await_bytes(packed.at[half, pl.ds(0, SIDE * SIDE - 1)], pack_send)
+
+    @pl.when(grid == branch)
+    def _():
+        await_bytes(extra.at[pl.ds(0, SIDE * SIDE - 1)], extra_send)
+
+    await_bytes(slots(core, 0, 0, 0, (RING - 1) * TILES), z_send)
+    await_bytes(slots(core, 0, 0, 0, RING * TILES), pair_send)
     for axis in (0, 1):
         far = lax.rem(place[axis] + 2, SIDE)
         await_bytes(gall.at[axis, far, 0], g_recv_sem.at[axis, 12])
@@ -473,17 +484,8 @@
 
     outs[2].start()
 
-    for copy in started:
+    for copy in started[-4:]:
         copy.wait_send()
-    for half in range(2):
-        await_bytes(packed.at[half, pl.ds(0, SIDE * SIDE - 1)], pack_send)
-
-    @pl.when(grid == branch)
-    def _():
-        await_bytes(extra.at[pl.ds(0, SIDE * SIDE - 1)], extra_send)
-
-    await_bytes(slots(core, 0, 0, 0, (RING - 1) * TILES), z_send)
-    await_bytes(slots(core, 0, 0, 0, RING * TILES), pair_send)
     for copy in outs:
         copy.wait()
 

time: 98.4 us -> 98.4 us (level)
  no operation moved by 1% of the time
where the time goes in v6:
time: 98.4 us; the launch traced here: 98.3 us
  Pallas kernels  97.7 us (99%)
    pallas_call x1, Pallas kernels, on_device(): pl.pallas_call(kernel, out_shape=(jax.ShapeDtypeStruct((NS1, SLICE, BS),...  95.6 us
    pallas_call x1, Pallas kernels, on_device(): pl.pallas_call(write_out, out_shape=(column, block, column, block, block)...  2.11 us

profile of v6, /device:TPU:1, one launch (start us, length us, event | category | flops | bytes accessed | tf_op | source)
XLA Modules:
  0.0 98.3 jit_solution(3744038536918627250)
XLA Ops:
  0.6 95.6 %shard_map.110 = (f32[12,16,256]{2,1,0:T(8,128)}, f32[12,16,256]{2,1,0:T(8,128)}, f32[3,256,256]{2,1,0:T(8,128)}) custom-call(s32[1,12]{1,0:T(1,128)} %struct_hbm.1, s32[1,6]{1,0:T(1,128)} %leaf_hbm.1, f32[512,512]{1,0:T(8,128)} %sigma_hbm.1, f32[1,256,256]{2,1,0:T(8,128)} %minv_hbm.1, f32[1,12,256,256]{3,2,1,0:T(8,128)} %moff_hbm.1, ...), custom_call_target="tpu_custom_call" | custom-call | tf_op jit(solution)/shard_map/pallas_call | solution.py:511
  96.2 2.1 %shard_map.111 = (f32[1,12,16,256]{3,2,1,0:T(8,128)}, f32[1,256,256]{2,1,0:T(8,128)}, f32[1,12,16,256]{3,2,1,0:T(8,128)}, f32[1,256,256]{2,1,0:T(8,128)}, f32[1,256,256]{2,1,0:T(8,128)}) custom-call(f32[12,16,256]{2,1,0:T(8,128)} %get-tuple-element.8.mid, f32[12,16,256]{2,1,0:T(8,128)} %get-tuple-element.9.leaf, f32[3,256,256]{2,1,0:T(8,128)} %get-tuple-element.10.gram), custom_call_target="tpu_custom_call" | custom-call | tf_op jit(solution)/shard_map/pallas_call | solution.py:575

commit v7 on v5

--- a/solution.py
+++ b/solution.py
@@ -411,17 +411,18 @@
     lax.fori_loop(0, 3, left_rows, 0)
     pack_rows(0, 1)
     first_hop(*y_ring(1))
+    put_gram(0, gram(0, 1) + gram(1, 0).T)
     h00 = gram(0, 0)
     h00 = h00 + h00.T
-    put_gram(0, h00[0:128])
-    put_gram(384, gram(0, 1) + gram(1, 0).T)
+    put_gram(256, h00[0:128])
+    first_hop(*g_ring(0))
+    direct_hop(*g_ring(0))
     h11 = gram(1, 1)
     h11 = h11 + h11.T
-    put_gram(128, h11[0:128])
-    put_gram(256, jnp.concatenate([h00[128:, 128:], h11[128:, 128:]], axis=1))
-    for axis in (0, 1):
-        first_hop(*g_ring(axis))
-        direct_hop(*g_ring(axis))
+    put_gram(384, h11[0:128])
+    put_gram(512, jnp.concatenate([h00[128:, 128:], h11[128:, 128:]], axis=1))
+    first_hop(*g_ring(1))
+    direct_hop(*g_ring(1))
     direct_hop(*y_ring(1))
     lax.fori_loop(0, 3, right_rows, 0)
     pack_rows(1, 0)
@@ -464,12 +465,12 @@
         await_bytes(gall.at[axis, far, 0], g_recv_sem.at[axis, 12])
         await_bytes(gall.at[axis, far, 1], g_recv_sem.at[axis, 13])
     total = gall[...].reshape(640, BS)
-    gram_out[1] = total[384:640] + base[1]
-    for index, first in ((0, 0), (2, 128)):
+    gram_out[1] = total[0:256] + base[1]
+    for index, first, side in ((0, 256, 0), (2, 384, 128)):
         upper = total[first:first + 128]
         gram_out[index, 0:128, :] = upper + base[index, 0:128, :]
         gram_out[index, 128:256, 0:128] = upper[:, 128:].T + base[index, 128:256, 0:128]
-        gram_out[index, 128:256, 128:256] = total[256:384, first:first + 128] + base[index, 128:256, 128:256]
+        gram_out[index, 128:256, 128:256] = total[512:640, side:side + 128] + base[index, 128:256, 128:256]
 
     outs[2].start()
 

time: 98.4 us -> 98.4 us (level)
  no operation moved by 1% of the time
where the time goes in v7:
time: 98.4 us; the launch traced here: 98.3 us
  Pallas kernels  97.7 us (99%)
    pallas_call x1, Pallas kernels, on_device(): pl.pallas_call(kernel, out_shape=(jax.ShapeDtypeStruct((NS1, SLICE, BS),...  95.6 us
    pallas_call x1, Pallas kernels, on_device(): pl.pallas_call(write_out, out_shape=(column, block, column, block, block)...  2.11 us

profile of v7, /device:TPU:1, one launch (start us, length us, event | category | flops | bytes accessed | tf_op | source)
XLA Modules:
  0.0 98.3 jit_solution(9190416404419874302)
XLA Ops:
  0.6 95.6 %shard_map.110 = (f32[12,16,256]{2,1,0:T(8,128)}, f32[12,16,256]{2,1,0:T(8,128)}, f32[3,256,256]{2,1,0:T(8,128)}) custom-call(s32[1,12]{1,0:T(1,128)} %struct_hbm.1, s32[1,6]{1,0:T(1,128)} %leaf_hbm.1, f32[512,512]{1,0:T(8,128)} %sigma_hbm.1, f32[1,256,256]{2,1,0:T(8,128)} %minv_hbm.1, f32[1,12,256,256]{3,2,1,0:T(8,128)} %moff_hbm.1, ...), custom_call_target="tpu_custom_call" | custom-call | tf_op jit(solution)/shard_map/pallas_call | solution.py:510
  96.2 2.1 %shard_map.111 = (f32[1,12,16,256]{3,2,1,0:T(8,128)}, f32[1,256,256]{2,1,0:T(8,128)}, f32[1,12,16,256]{3,2,1,0:T(8,128)}, f32[1,256,256]{2,1,0:T(8,128)}, f32[1,256,256]{2,1,0:T(8,128)}) custom-call(f32[12,16,256]{2,1,0:T(8,128)} %get-tuple-element.8.mid, f32[12,16,256]{2,1,0:T(8,128)} %get-tuple-element.9.leaf, f32[3,256,256]{2,1,0:T(8,128)} %get-tuple-element.10.gram), custom_call_target="tpu_custom_call" | custom-call | tf_op jit(solution)/shard_map/pallas_call | solution.py:574
